TPU v7x, 32 devices: a whole 2x2x4 slice. The times are simulated.
32 devices in a mesh: slab: 16 (over z, x, core), plane: 2 (over y).
Axes of the slice: x: 2, y: 2, z: 4, core: 2. Of those that a mesh axis runs over, the one named last changes fastest.
Arguments:
- probe_pos: bfloat16 [3, 4096], P(None, ('slab', 'plane')), may hold values from 0 to 2
- atom_pos: bfloat16 [3, 4096], P(None, ('slab', 'plane')), may hold values from 0 to 2
- atom_feat: bfloat16 [128, 4096], P(None, ('slab', 'plane')), may hold values from -6 to 6
- neighbours: int32 [32, 4096], P(None, ('slab', 'plane')), may hold values from 0 to 4095, as said below
- valid: int32 [32, 4096], P(None, ('slab', 'plane')), may hold values 0 or 1
- w_radial1: float32 [64, 8], replicated, may hold values from -2 to 2
- w_radial2: bfloat16 [640, 64], replicated, may hold values from -0.75 to 0.75
- readout: float32 [5, 128], replicated, may hold values from -0.5 to 0.5
- cotangent: float32 [4096], P(('slab', 'plane')), may hold values from -6 to 6
Outputs:
- density: float32 [4096], P(('slab', 'plane'))
- grad_feat: float32 [128, 4096], P(None, ('slab', 'plane'))
- grad_radial1: float32 [64, 8], replicated
- grad_radial2: float32 [640, 64], replicated
- grad_readout: float32 [5, 128], replicated
Inputs may be any that keep to these rules, and one draw needn't show every extreme that they name: `neighbours`: the atom of every slot of probe p lies in the slab of p (atoms a with a // 256 = p // 256) or in one of the two slabs beside it on the periodic cycle of slabs.
All inputs are finite; a program needn't handle non-finite values. No bound on the sum of `valid` on one device may be relied on, other than what follows from the above.
Results may differ from a plain program's by a relative error of at most 0.0049.
Values may be sent and summed in bfloat16 or wider, within the bound.
A program may use at most 128 MiB of HBM per device.

v0:
```python
import math

import jax
import jax.numpy as jnp
from jax import lax
from jax.sharding import PartitionSpec as P

slab_width = 2.0
soften = 0.25


def padded(block, sides, width):
    for axis, dim in sides:
        count = lax.axis_size(axis)
        forward = [(i, i + 1) for i in range(count - 1)]
        forward.append((count - 1, 0))
        backward = [(target, source) for source, target in forward]
        low = lax.ppermute(
            lax.slice_in_dim(block, block.shape[dim] - width, None, axis=dim), axis, forward
        )
        high = lax.ppermute(lax.slice_in_dim(block, 0, width, axis=dim), axis, backward)
        block = jnp.concatenate([low, block, high], axis=dim)
    return block


def passed_along(block, axis, distance):
    devices = range(lax.axis_size(axis))
    route = [((i - distance) % len(devices), i) for i in devices]
    return lax.ppermute(block, axis, route)


def harmonics(along_x, along_y, along_z):
    sq_x = along_x * along_x
    sq_y = along_y * along_y
    sq_z = along_z * along_z
    root3 = math.sqrt(3.0)
    root15 = math.sqrt(15.0)
    root5 = math.sqrt(5.0)
    coef_a1 = math.sqrt(35.0 / 8.0)
    coef_a2 = math.sqrt(105.0)
    coef_a3 = math.sqrt(21.0 / 8.0)
    coef_a4 = math.sqrt(7.0) / 2.0
    coef_b1 = 3.0 * math.sqrt(35.0) / 2.0
    coef_b2 = 3.0 * math.sqrt(70.0) / 4.0
    coef_b3 = 3.0 * math.sqrt(5.0) / 2.0
    coef_b4 = 3.0 * math.sqrt(10.0) / 4.0
    rows_out = [
        jnp.ones_like(along_x),
        root3 * along_y,
        root3 * along_z,
        root3 * along_x,
        root15 * along_x * along_y,
        root15 * along_y * along_z,
        root5 / 2.0 * (3.0 * sq_z - 1.0),
        root15 * along_x * along_z,
        root15 / 2.0 * (sq_x - sq_y),
        coef_a1 * along_y * (3.0 * sq_x - sq_y),
        coef_a2 * along_x * along_y * along_z,
        coef_a3 * along_y * (5.0 * sq_z - 1.0),
        coef_a4 * along_z * (5.0 * sq_z - 3.0),
        coef_a3 * along_x * (5.0 * sq_z - 1.0),
        coef_a2 / 2.0 * along_z * (sq_x - sq_y),
        coef_a1 * along_x * (sq_x - 3.0 * sq_y),
        coef_b1 * along_x * along_y * (sq_x - sq_y),
        coef_b2 * along_y * along_z * (3.0 * sq_x - sq_y),
        coef_b3 * along_x * along_y * (7.0 * sq_z - 1.0),
        coef_b4 * along_y * along_z * (7.0 * sq_z - 3.0),
        0.375 * (35.0 * sq_z * sq_z - 30.0 * sq_z + 3.0),
        coef_b4 * along_x * along_z * (7.0 * sq_z - 3.0),
        coef_b3 / 2.0 * (sq_x - sq_y) * (7.0 * sq_z - 1.0),
        coef_b2 * along_x * along_z * (sq_x - 3.0 * sq_y),
        coef_b1 / 4.0 * (sq_x * (sq_x - 3.0 * sq_y) - sq_y * (3.0 * sq_x - sq_y)),
    ]
    return jnp.stack(rows_out)


def probe_block(
    features, atom_xyz, probe_xyz, offset, weight_mask, cot_block, w_radial1, w_radial2, readout
):
    slots, block_len = weight_mask.shape
    edge_count = slots * block_len
    channels = features.shape[0]
    degrees = readout.shape[0]
    probe_tile = jnp.broadcast_to(probe_xyz[:, None, :], (3, slots, block_len)).reshape(
        3, edge_count
    )
    delta_x = atom_xyz[0] - probe_tile[0]
    delta_y = atom_xyz[1] - probe_tile[1]
    delta_z = atom_xyz[2] + slab_width * offset.reshape(edge_count) - probe_tile[2]
    radius = jnp.sqrt(delta_x * delta_x + delta_y * delta_y + delta_z * delta_z + soften)
    sphere = harmonics(delta_x / radius, delta_y / radius, delta_z / radius)
    centres = 0.75 * jnp.arange(w_radial1.shape[1], dtype=jnp.float32)
    radial_basis = jnp.exp(-2.0 * (radius[None, :] - centres[:, None]) ** 2)
    preact = jnp.dot(w_radial1, radial_basis, precision=lax.Precision.HIGHEST)
    hidden = jax.nn.silu(preact).astype(jnp.bfloat16)
    radial = jnp.dot(w_radial2, hidden, preferred_element_type=jnp.float32).reshape(
        degrees, channels, edge_count
    )
    weight = weight_mask.reshape(edge_count) * (1.0 / math.sqrt(slots))
    feat_float = features.astype(jnp.float32)
    messages = (radial * feat_float[None] * weight[None, None, :]).reshape(
        degrees, channels, slots, block_len
    )
    sphere_rows = sphere.reshape(degrees * degrees, slots, block_len)
    density = jnp.zeros((block_len,), jnp.float32)
    grad_msg = []
    grad_read = []
    for degree in range(degrees):
        part_y = sphere_rows[degree * degree : (degree + 1) * (degree + 1)]
        moment = jnp.einsum(
            "kjp,cjp->kcp", part_y, messages[degree], precision=lax.Precision.HIGHEST
        )
        if degree == 0:
            density = jnp.sum(readout[0][:, None] * moment[0], axis=0)
            grad_mom = cot_block[None, None, :] * readout[0][None, :, None]
            grad_read.append(jnp.sum(cot_block[None, :] * moment[0], axis=1))
        else:
            squares = jnp.sum(moment * moment, axis=0)
            density = density + jnp.sum(readout[degree][:, None] * squares, axis=0)
            grad_mom = 2.0 * cot_block[None, None, :] * readout[degree][None, :, None] * moment
            grad_read.append(jnp.sum(cot_block[None, :] * squares, axis=1))
        grad_msg.append(
            jnp.einsum("kjp,kcp->cjp", part_y, grad_mom, precision=lax.Precision.HIGHEST)
        )
    grad_messages = jnp.stack(grad_msg).reshape(degrees, channels, edge_count)
    grad_features = jnp.sum(grad_messages * radial, axis=0) * weight[None, :]
    grad_radial = (
        (grad_messages * feat_float[None] * weight[None, None, :])
        .reshape(degrees * channels, edge_count)
        .astype(jnp.bfloat16)
    )
    grad_w2 = lax.dot_general(
        grad_radial, hidden, (((1,), (1,)), ((), ())), preferred_element_type=jnp.float32
    )
    grad_hidden = lax.dot_general(
        w_radial2, grad_radial, (((0,), (0,)), ((), ())), preferred_element_type=jnp.float32
    )
    logistic = jax.nn.sigmoid(preact)
    grad_pre = grad_hidden * logistic * (1.0 + preact * (1.0 - logistic))
    grad_w1 = lax.dot_general(
        grad_pre, radial_basis, (((1,), (1,)), ((), ())), precision=lax.Precision.HIGHEST
    )
    return (density, grad_features, grad_w1, grad_w2, jnp.stack(grad_read))


def shards(
    probe_pos, atom_pos, atom_feat, neighbours, valid, w_radial1, w_radial2, readout, cotangent
):
    channels = atom_feat.shape[0]
    atom_dev = atom_feat.shape[1]
    plane_count = lax.axis_size("plane")
    slab_count = lax.axis_size("slab")
    slab_index = lax.axis_index("slab")
    atom_slab = atom_dev * plane_count
    atom_pack = jnp.concatenate([atom_feat, atom_pos], axis=0)
    slab_pack = lax.all_gather(atom_pack, "plane", axis=1, tiled=True)
    window = padded(slab_pack, (("slab", 1),), atom_slab)
    window_feat = window[:channels]
    window_xyz = window[channels:]
    local_rows = (neighbours - (slab_index - 1) * atom_slab) % (slab_count * atom_slab)
    offsets = (local_rows // atom_slab - 1).astype(jnp.float32)
    slots, probe_dev = neighbours.shape
    block_len = 128
    count = probe_dev // block_len
    rows_blocks = local_rows.reshape(slots, count, block_len).transpose(1, 0, 2)
    offset_blocks = offsets.reshape(slots, count, block_len).transpose(1, 0, 2)
    mask_blocks = valid.astype(jnp.float32).reshape(slots, count, block_len).transpose(1, 0, 2)
    probe_blocks = probe_pos.astype(jnp.float32).reshape(3, count, block_len).transpose(1, 0, 2)
    cot_blocks = cotangent.reshape(count, block_len)

    def advance(totals, inputs):
        grad_window, total_w1, total_w2, total_read = totals
        atom_rows, offset, mask_float, probe_xyz, cot_block = inputs
        flat_rows = atom_rows.reshape(-1)
        features = jnp.take(window_feat, flat_rows, axis=1)
        atom_xyz = jnp.take(window_xyz, flat_rows, axis=1).astype(jnp.float32)
        density, grad_features, grad_w1, grad_w2, grad_read = probe_block(
            features,
            atom_xyz,
            probe_xyz,
            offset,
            mask_float,
            cot_block,
            w_radial1,
            w_radial2,
            readout,
        )
        grad_window = grad_window.at[:, flat_rows].add(grad_features)
        return (
            (grad_window, total_w1 + grad_w1, total_w2 + grad_w2, total_read + grad_read),
            density,
        )

    start_totals = (
        jnp.zeros((channels, 3 * atom_slab), jnp.float32),
        jnp.zeros(w_radial1.shape, jnp.float32),
        jnp.zeros(w_radial2.shape, jnp.float32),
        jnp.zeros(readout.shape, jnp.float32),
    )
    totals, densities = lax.scan(
        advance, start_totals, (rows_blocks, offset_blocks, mask_blocks, probe_blocks, cot_blocks)
    )
    grad_window = totals[0]
    window_parts = grad_window.reshape(channels, 3, plane_count, atom_dev)
    own_share = lax.psum_scatter(window_parts, "plane", scatter_dimension=2, tiled=True).reshape(
        channels, 3, atom_dev
    )
    lower_part = passed_along(own_share[:, 0], "slab", -1)
    upper_part = passed_along(own_share[:, 2], "slab", 1)
    grad_feat = own_share[:, 1] + lower_part + upper_part
    summed_w1, summed_w2, summed_read = lax.psum(
        (totals[1], totals[2], totals[3]), ("slab", "plane")
    )
    scale = 1.0 / math.sqrt(probe_dev * slab_count * plane_count)
    return (
        densities.reshape(-1),
        grad_feat,
        summed_w1 * scale,
        summed_w2 * scale,
        summed_read * scale,
    )


def solution(mesh):
    in_specs = (
        P(None, ("slab", "plane")),
        P(None, ("slab", "plane")),
        P(None, ("slab", "plane")),
        P(None, ("slab", "plane")),
        P(None, ("slab", "plane")),
        P(),
        P(),
        P(),
        P(("slab", "plane")),
    )
    out_specs = (P(("slab", "plane")), P(None, ("slab", "plane")), P(), P(), P())
    return jax.shard_map(shards, mesh=mesh, in_specs=in_specs, out_specs=out_specs, check_vma=False)
```

profile of v0, /device:TPU:8, one launch (start us, length us, event | category | flops | bytes accessed | tf_op | source)
XLA Modules:
  0.0 372.6 jit_solution(13658433826275960713)
XLA Ops:
  9.8 4.9 %all_gather.3 = bf16[131,256]{0,1:T(8,128)(2,1)S(1)} all-gather(bf16[131,128]{0,1:T(8,128)(2,1)S(1)} %pad_maximum_fusion), channel_id=1, replica_groups=mesh['slab'=16,'plane'=2] {'plane'}, dimensions={1}, use_global_device_ids=true | all-gather | bytes 100608 | tf_op jit(solution)/shard_map/all_gather | solution.py:156
  22.4 12.1 %gather_fusion = bf16[4096,3]{1,0:T(8,128)(2,1)S(1)} fusion(bf16[3,768]{0,1:T(8,128)(2,1)S(1)} %slice.163, s32[4096]{0:T(1024)S(1)} %broadcast_clamp_fusion), kind=kCustom, calls=%fused_computation | custom fusion | bytes 65536 | tf_op jit(solution)/shard_map/while/body/eval_jaxpr/jit(_take)/gather | solution.py:176
  39.3 5.4 %fusion.60 = f32[4096,640]{0,1:T(8,128)} fusion(bf16[640,64]{0,1:T(8,128)(2,1)S(1)} %copy-done, f32[64,4096]{1,0:T(8,128)S(1)} %convolution_bitcast_fusion.1), kind=kOutput, calls=%fused_computation.170 | convolution fusion | flops 336855040 | bytes 11616256 | tf_op jit(solution)/shard_map/while/body/eval_jaxpr/dot_general | solution.py:96
  44.7 11.3 %copy.168 = f32[5,128,4096]{1,2,0:T(8,128)} copy(f32[5,128,4096]{2,1,0:T(8,128)} %bitcast.137) | data formatting | bytes 20971520 | tf_op jit(solution)/shard_map/while/body/eval_jaxpr/reshape | solution.py:96
  56.0 14.9 %gather_fusion.1 = bf16[4096,128]{1,0:T(8,128)(2,1)} fusion(bf16[128,768]{0,1:T(8,128)(2,1)S(1)} %slice.167, s32[4096]{0:T(1024)S(1)} %broadcast_clamp_fusion), kind=kCustom, calls=%fused_computation.1 | custom fusion | bytes 2113536 | tf_op jit(solution)/shard_map/while/body/eval_jaxpr/jit(_take)/gather | solution.py:175
  70.9 3.4 convert_bitcast_fusion
  74.3 6.1 %multiply_multiply_fusion = f32[5,128,4096]{1,2,0:T(8,128)S(1)} fusion(f32[5,128,4096]{1,2,0:T(8,128)} %copy.168, f32[4096]{0:T(1024)S(1)} %multiply_bitcast_fusion.1, f32[128,4096]{0,1:T(8,128)S(1)} %convert_bitcast_fusion), kind=kLoop, calls=%fused_computation.6 | loop fusion | flops 5242880 | bytes 23085056 | tf_op jit(solution)/shard_map/while/body/eval_jaxpr/mul | solution.py:101
  80.4 4.0 %fusion.62 = (f32[1,128,4096]{1,2,0:T(8,128)}, f32[1,128,4096]{1,2,0:T(8,128)}, f32[1,128,4096]{1,2,0:T(8,128)}, f32[1,128,4096]{1,2,0:T(8,128)}, f32[1,128,4096]{1,2,0:T(8,128)}) fusion(f32[5,128,4096]{1,2,0:T(8,128)S(1)} %multiply_multiply_fusion), kind=kLoop, calls=%fused_computation.171 | loop fusion | bytes 20971520 | tf_op jit(solution)/shard_map/while/body/eval_jaxpr/slice | solution.py:111
  84.4 5.2 %fusion.5 = f32[128,1,128]{2,1,0:T(1,128)} fusion(f32[128,32,128]{0,2,1:T(8,128)} %bitcast.142), kind=kOutput, calls=%fused_computation.14 | convolution fusion | flops 6291456 | bytes 2162688 | tf_op jit(solution)/shard_map/while/body/eval_jaxpr/kjp,cjp->kcp/dot_general | solution.py:110
  99.9 4.8 %multiply_reduce_fusion.1 = (f32[128,128]{0,1:T(8,128)S(1)}, f32[9,128,128]{1,0,2:T(8,128)S(1)}) fusion(f32[9,32,128]{1,0,2:T(8,128)S(1)} %copy.176, f32[128,32,128]{0,2,1:T(8,128)} %bitcast.141), kind=kOutput, calls=%fused_computation.36 | convolution fusion | flops 56901632 | bytes 2899968 | tf_op jit(solution)/shard_map/while/body/eval_jaxpr/kjp,cjp->kcp/dot_general | solution.py:110
  104.8 3.1 multiply_reduce_fusion.4
  108.0 3.3 multiply_reduce_fusion.3
  111.3 3.1 multiply_reduce_fusion.2
  115.2 3.5 convolution_bitcast_fusion.5
  119.8 3.7 convolution_bitcast_fusion.4
  124.7 3.5 convolution_bitcast_fusion.3
  129.4 3.5 convolution_bitcast_fusion.2
  137.2 7.5 %broadcast_multiply_fusion = (f32[5,128,4096]{1,2,0:T(8,128)}, f32[128,4096]{0,1:T(8,128)}) fusion(f32[5,128,4096]{1,2,0:T(8,128)S(1)} %constant_dynamic-update-slice_fusion.3, f32[128,4096]{0,1:T(8,128)S(1)} %convert_bitcast_fusion, f32[5,128,4096]{1,2,0:T(8,128)S(1)} %bitcast.136), kind=kLoop, calls=%fused_computation.7 | loop fusion | flops 7340032 | bytes 35651584 | tf_op jit(solution)/shard_map/while/body/eval_jaxpr/mul | solution.py:128
  144.7 24.9 %scatter_custom_fusion = f32[128,768]{0,1:T(8,128)S(1)} fusion(s32[4096]{0:T(1024)} %bitcast.169, f32[128,4096]{0,1:T(8,128)} %get-tuple-element.85, f32[4096]{0:T(1024)S(1)} %multiply_bitcast_fusion.1, f32[]{:T(128)} %constant.170.clone.1), kind=kCustom, calls=%fused_computation.12 | custom fusion | flops 1048576 | bytes 2507264 | tf_op jit(solution)/shard_map/while/body/eval_jaxpr/scatter-add | solution.py:188
  170.6 11.3 %copy.187 = f32[5,128,4096]{2,1,0:T(8,128)} copy(f32[5,128,4096]{1,2,0:T(8,128)} %get-tuple-element.84) | data formatting | bytes 20971520 | tf_op jit(solution)/shard_map/while/body/eval_jaxpr/mul | solution.py:128
  181.8 5.4 %fusion = bf16[640,4096]{1,0:T(8,128)(2,1)S(1)} fusion(f32[5,128,4096]{2,1,0:T(8,128)} %copy.187, f32[4096]{0:T(1024)S(1)} %multiply_bitcast_fusion.1), kind=kLoop, calls=%fused_computation.4 | loop fusion | flops 5242880 | bytes 15745024 | tf_op jit(solution)/shard_map/while/body/eval_jaxpr/convert_element_type | solution.py:130
  190.6 39.7 %all-reduce = (f32[64,8]{0,1:T(8,128)S(1)}, f32[5,128]{1,0:T(8,128)S(1)}) all-reduce(f32[64,8]{0,1:T(8,128)S(1)} %fusion.38, f32[5,128]{1,0:T(8,128)S(1)} %stack.121), channel_id=1, replica_groups=mesh['slab'=16,'plane'=2] {'slab','plane'}, use_global_device_ids=true, to_apply=%region_12.13 | all-reduce | flops 1152 | bytes 9216 | tf_op jit(solution)/shard_map/psum | solution.py:211
  231.5 4.9 %fusion.59 = f32[640,64]{0,1:T(8,128)} fusion(bf16[640,4096]{1,0:T(8,128)(2,1)} %copy-done.6, f32[64,4096]{1,0:T(8,128)S(1)} %copy-done.5), kind=kOutput, calls=%fused_computation.169 | convolution fusion | flops 336855040 | bytes 6455296 | tf_op jit(solution)/shard_map/while/body/eval_jaxpr/dot_general | solution.py:132
  240.5 121.1 %all-reduce.3.cloned.1.call-done = f32[640,64]{0,1:T(8,128)} async-done(((f32[640,64]{0,1:T(8,128)}), f32[640,64]{0,1:T(8,128)}) %all-reduce.3.cloned.1.call-update) | async-done | bytes 163856 | tf_op jit(solution)/shard_map/psum | solution.py:211
  (127 shorter events, 45.5 us)
Async XLA Ops:
  8.0 31.3 %copy-start = (bf16[640,64]{0,1:T(8,128)(2,1)S(1)}, bf16[640,64]{0,1:T(8,128)(2,1)}, u32[]{:S(2)}) copy-start(bf16[640,64]{0,1:T(8,128)(2,1)} %param.15) | copy-start | bytes 245764
  8.0 228.9 %reduce-scatter.2.cloned.1.call-start = ((), (), s32[]{:S(2)}) async-start(), calls=%async_computation.1 | async-start | bytes 589824 | tf_op jit(solution)/shard_map/reduce_scatter | solution.py:205
  14.7 7.6 %collective-permute-start = (bf16[131,256]{0,1:T(8,128)(2,1)S(1)}, bf16[131,256]{0,1:T(8,128)(2,1)S(1)}, u32[]{:S(2)}, u32[]{:S(2)}) collective-permute-start(bf16[131,256]{0,1:T(8,128)(2,1)S(1)} %all_gather.3), channel_id=1, source_target_pairs={{0,2},{2,4},{4,6},{6,8},{8,10},{10,12},{12,14},{14,16},{16,18},{18... | collective-permute-start | bytes 201224 | tf_op jit(solution)/shard_map/ppermute | solution.py:18
  14.7 7.6 %collective-permute-start.1 = (bf16[131,256]{0,1:T(8,128)(2,1)S(1)}, bf16[131,256]{0,1:T(8,128)(2,1)S(1)}, u32[]{:S(2)}, u32[]{:S(2)}) collective-permute-start(bf16[131,256]{0,1:T(8,128)(2,1)S(1)} %all_gather.3), channel_id=1, source_target_pairs={{2,0},{4,2},{6,4},{8,6},{10,8},{12,10},{14,12},{16,14},{18,16},{20... | collective-permute-start | bytes 201224 | tf_op jit(solution)/shard_map/ppermute | solution.py:21
  18.8 3.5 copy-start.12
  22.3 16.0 %copy-start.14 = (f32[8]{0:T(128)}, f32[8]{0:T(128)S(1)}, u32[]{:S(2)}) copy-start(f32[8]{0:T(128)S(1)} %iota_multiply_fusion) | copy-start | bytes 100
  34.5 3.7 %copy-start.13 = (f32[64,8]{0,1:T(8,128)S(1)}, f32[64,8]{0,1:T(8,128)}, u32[]{:S(2)}) copy-start(f32[64,8]{0,1:T(8,128)} %param.14) | copy-start | bytes 6148
  36.5 8.3 %copy-start.10 = (f32[1,4096]{1,0:T(1,128)}, f32[1,4096]{1,0:T(1,128)S(1)}, u32[]{:S(2)}) copy-start(f32[1,4096]{1,0:T(1,128)S(1)} %get-tuple-element.125) | copy-start | bytes 49156
  39.3 5.4 %copy-start.4 = (f32[64,4096]{1,0:T(8,128)}, f32[64,4096]{1,0:T(8,128)S(1)}, u32[]{:S(2)}) copy-start(f32[64,4096]{1,0:T(8,128)S(1)} %convolution_bitcast_fusion.1) | copy-start | bytes 3145732
  99.9 4.9 %copy-start.3 = (f32[1,128,4096]{1,2,0:T(8,128)S(1)}, f32[1,128,4096]{1,2,0:T(8,128)}, u32[]{:S(2)}) copy-start(f32[1,128,4096]{1,2,0:T(8,128)} %get-tuple-element.89) | copy-start | bytes 6291460
  107.9 3.4 copy-start.1
  107.9 3.4 copy-start.8
  111.2 3.2 copy-start.9
  111.2 3.2 copy-start.16
  111.3 3.2 copy-start.17
  111.3 3.2 copy-start.18
  111.3 3.2 copy-start.19
  111.3 3.2 copy-start.20
  111.3 3.2 copy-start.21
  111.3 3.2 copy-start.22
  170.5 191.1 %all-reduce.3.cloned.1.call-start = ((), (), s32[]{:S(2)}) async-start(), calls=%async_computation.2 | async-start | bytes 327680 | tf_op jit(solution)/shard_map/psum | solution.py:211
  181.8 5.4 %copy-start.5 = (f32[64,4096]{1,0:T(8,128)S(1)}, f32[64,4096]{1,0:T(8,128)}, u32[]{:S(2)}) copy-start(f32[64,4096]{1,0:T(8,128)} %copy-done.4) | copy-start | bytes 3145732
  237.8 125.4 %collective-permute-start.3 = (f32[128,128]{1,0:T(8,128)S(1)}, f32[128,128]{1,0:T(8,128)S(1)}, u32[]{:S(2)}, u32[]{:S(2)}) collective-permute-start(f32[128,128]{1,0:T(8,128)S(1)} %get-tuple-element.92), channel_id=1, source_target_pairs={{30,0},{0,2},{2,4},{4,6},{6,8},{8,10},{10,12},{12,14},{14,16},{16,... | collective-permute-start | bytes 196616 | tf_op jit(solution)/shard_map/ppermute | solution.py:29
  237.9 125.3 %collective-permute-start.2 = (f32[128,128]{1,0:T(8,128)S(1)}, f32[128,128]{1,0:T(8,128)S(1)}, u32[]{:S(2)}, u32[]{:S(2)}) collective-permute-start(f32[128,128]{1,0:T(8,128)S(1)} %get-tuple-element.91), channel_id=1, source_target_pairs={{2,0},{4,2},{6,4},{8,6},{10,8},{12,10},{14,12},{16,14},{18,16},{20... | collective-permute-start | bytes 196616 | tf_op jit(solution)/shard_map/ppermute | solution.py:29
  (8 other events, 20.3 us)
Sparse Core Ops, SparseCore 0:
  170.6 13.6 reduce-scatter.1
Sparse Core Ops, SparseCore 1:
  236.5 125.1 all-reduce.2
where the time goes:
time: 379 us; the launch traced here: 373 us
  waiting for transfers between devices  121 us (32%)
  local copies, waits for them, and re-layouts  79.4 us (21%)
  other arithmetic  58.3 us (15%)
  matrix products  47 us (12%)
  blocking collectives  44.6 us (12%)
  between operations  16.6 us (4%)
  starting transfers between devices  5.42 us (1%)
    psum x1, waiting for transfers between devices, shards(): lax.psum((totals[1], totals[2], totals[3]), ('slab', 'plane'))  121 us
    psum x1, blocking collectives, shards(): lax.psum((totals[1], totals[2], totals[3]), ('slab', 'plane'))  39.7 us
    scatter-add x1, other arithmetic, advance(): grad_window = grad_window.at[:, flat_rows].add(grad_features)  24.9 us
    dot_general x5, matrix products, probe_block(): jnp.einsum('kjp,cjp->kcp', part_y, messages[degree], precision=lax.Precis...  19.5 us
    gather x1, local copies, waits for them, and re-layouts, advance(): features = jnp.take(window_feat, flat_rows, axis=1)  14.9 us
    dot_general x4, matrix products, probe_block(): jnp.einsum('kjp,kcp->cjp', part_y, grad_mom, precision=lax.Precision.HIGH...  14.1 us
    gather x2, local copies, waits for them, and re-layouts, advance(): atom_xyz = jnp.take(window_xyz, flat_rows, axis=1).astype(jnp.float32)  12.5 us
    mul x1, local copies, waits for them, and re-layouts, probe_block(): grad_messages * feat_float[None] * weight[None, None, :]  11.3 us
  transfers between devices with their start and end apart: 6, of which 1 were waited for; matrix products, arithmetic and copies ran while one was open for 9% of the time, Pallas kernels for 0%

commit v1 on v0

v1 whole, which is shorter than its diff:
```python
import functools
import math

import jax
import jax.numpy as jnp
from jax import lax
from jax.experimental import pallas as pl
from jax.experimental.pallas import tpu as pltpu
from jax.sharding import PartitionSpec as P

slab_width = 2.0
soften = 0.25
f32 = jnp.float32
bf16 = jnp.bfloat16
MESH = pl.DeviceIdType.MESH
HIGH = lax.Precision.HIGHEST
VMEM = pl.BlockSpec(memory_space=pltpu.VMEM)
NT = (((1,), (1,)), ((), ()))
TN = (((0,), (0,)), ((), ()))


def harmonics(x, y, z):
    xx, yy, zz = x * x, y * y, z * z
    r3, r5, r15 = math.sqrt(3.0), math.sqrt(5.0), math.sqrt(15.0)
    a1, a2 = math.sqrt(35.0 / 8.0), math.sqrt(105.0)
    a3, a4 = math.sqrt(21.0 / 8.0), math.sqrt(7.0) / 2.0
    b1, b2 = 3.0 * math.sqrt(35.0) / 2.0, 3.0 * math.sqrt(70.0) / 4.0
    b3, b4 = 3.0 * math.sqrt(5.0) / 2.0, 3.0 * math.sqrt(10.0) / 4.0
    return [
        jnp.ones_like(x),
        r3 * y,
        r3 * z,
        r3 * x,
        r15 * x * y,
        r15 * y * z,
        r5 / 2.0 * (3.0 * zz - 1.0),
        r15 * x * z,
        r15 / 2.0 * (xx - yy),
        a1 * y * (3.0 * xx - yy),
        a2 * x * y * z,
        a3 * y * (5.0 * zz - 1.0),
        a4 * z * (5.0 * zz - 3.0),
        a3 * x * (5.0 * zz - 1.0),
        a2 / 2.0 * z * (xx - yy),
        a1 * x * (xx - 3.0 * yy),
        b1 * x * y * (xx - yy),
        b2 * y * z * (3.0 * xx - yy),
        b3 * x * y * (7.0 * zz - 1.0),
        b4 * y * z * (7.0 * zz - 3.0),
        0.375 * (35.0 * zz * zz - 30.0 * zz + 3.0),
        b4 * x * z * (7.0 * zz - 3.0),
        b3 / 2.0 * (xx - yy) * (7.0 * zz - 1.0),
        b2 * x * z * (xx - 3.0 * yy),
        b1 / 4.0 * (xx * (xx - 3.0 * yy) - yy * (3.0 * xx - yy)),
    ]


def halo_peers(n_slab, n_plane):
    slab, plane = lax.axis_index("slab"), lax.axis_index("plane")
    peers = []
    for d in (-1, 0, 1):
        for q in range(n_plane):
            if d == 0 and q == 0:
                continue
            to_slab = lax.rem(slab + d + n_slab, n_slab)
            to_plane = lax.rem(plane + q, n_plane)
            peers.append((d, q, to_slab, to_plane))
    return slab, plane, peers


def halo_kernel(n_slab, n_plane, own_ref, out_ref, land, send_sem, recv_sem):
    slab, plane, peers = halo_peers(n_slab, n_plane)
    barrier = pltpu.get_barrier_semaphore()
    for _, _, to_slab, to_plane in peers:
        pl.semaphore_signal(barrier, inc=1, device_id=(to_slab, to_plane), device_id_type=MESH)
    pl.semaphore_wait(barrier, len(peers))
    copies = []
    for number, (d, _, to_slab, to_plane) in enumerate(peers):
        copy = pltpu.make_async_remote_copy(
            src_ref=own_ref,
            dst_ref=land.at[(1 - d) * n_plane + plane],
            send_sem=send_sem.at[number],
            recv_sem=recv_sem.at[number],
            device_id=(to_slab, to_plane),
            device_id_type=MESH,
        )
        copy.start()
        copies.append(copy)
    land[n_plane + plane] = own_ref[...]
    for copy in copies:
        copy.wait()
    out_ref[...] = land[...]


def edge_kernel(
    n_slab,
    n_plane,
    win_ref,
    nbr_ref,
    valid_ref,
    probe_ref,
    cot_ref,
    w1_ref,
    w2_ref,
    read_ref,
    readt_ref,
    dens_ref,
    gwin_ref,
    pack_ref,
    win,
    rows_s,
    wgt,
    xyz,
    onehot,
    feat,
    gfeat,
    sph,
    sphb,
    rad_s,
    basis,
    pre,
    hid,
    radial,
    gradial,
    squares,
    gwin_acc,
    gw2_acc,
    gw1_acc,
):
    slots, probes = nbr_ref.shape
    blocks, _, atoms = win_ref.shape
    width = blocks * atoms
    atom_slab = n_plane * atoms
    channels = feat.shape[0]
    degrees = read_ref.shape[0]
    per = 4
    chunk = per * probes
    chunks = slots // per
    total = n_slab * atom_slab
    for b in range(blocks):
        win[:, b * atoms : (b + 1) * atoms] = win_ref[b]
    local = nbr_ref[...] - (lax.axis_index("slab") - 1) * atom_slab
    local = jnp.where(local < 0, local + total, local)
    local = jnp.where(local >= total, local - total, local)
    rows_s[...] = local
    wgt[...] = valid_ref[...].astype(f32) * (1.0 / math.sqrt(slots))
    offset = jnp.where(local < atom_slab, -1.0, jnp.where(local < 2 * atom_slab, 0.0, 1.0))
    atom_iota = lax.broadcasted_iota(jnp.int32, (width, probes), 0)

    def gather(i, _):
        for s in range(per):
            row = rows_s[pl.ds(i * per + s, 1), :]
            at = pl.multiple_of(i * chunk + s * probes, probes)
            onehot[:, pl.ds(at, probes)] = (atom_iota == row).astype(f32).astype(bf16)
        at = pl.multiple_of(i * chunk, chunk)
        got = jnp.dot(win[...], onehot[:, pl.ds(at, chunk)], preferred_element_type=f32)
        for s in range(per):
            j = i * per + s
            part = got[:, s * probes : (s + 1) * probes]
            at = pl.multiple_of(i * chunk + s * probes, probes)
            feat[:, pl.ds(at, probes)] = part[:channels] * wgt[pl.ds(j, 1), :]
            for k in range(3):
                xyz[k, pl.ds(j, 1), :] = part[channels + k : channels + k + 1]
        return 0

    lax.fori_loop(0, chunks, gather, 0)

    probe = probe_ref[...].astype(f32)
    dx = xyz[0] - probe[0:1]
    dy = xyz[1] - probe[1:2]
    dz = xyz[2] + slab_width * offset - probe[2:3]
    radius = jnp.sqrt(dx * dx + dy * dy + dz * dz + soften)
    rad_s[...] = radius
    for k, row in enumerate(harmonics(dx / radius, dy / radius, dz / radius)):
        sph[k] = row
    rows_k = degrees * degrees
    sph[rows_k] = wgt[...]

    n_basis = w1_ref.shape[1]
    centres = 0.75 * lax.broadcasted_iota(jnp.int32, (n_basis, probes), 0).astype(f32)

    def spread(j, _):
        for k in range(rows_k + 1):
            sphb[j, k] = jnp.broadcast_to(sph[k, pl.ds(j, 1), :], (8, probes))
        shift = rad_s[pl.ds(j, 1), :] - centres
        basis[:, pl.ds(pl.multiple_of(j * probes, probes), probes)] = jnp.exp(
            -2.0 * (shift * shift)
        )
        return 0

    lax.fori_loop(0, slots, spread, 0)

    def network(i, _):
        at = pl.ds(pl.multiple_of(i * chunk, chunk), chunk)
        value = jnp.dot(w1_ref[...], basis[:, at], precision=HIGH, preferred_element_type=f32)
        pre[:, at] = value
        hidden = (value * jax.nn.sigmoid(value)).astype(bf16)
        hid[:, at] = hidden
        radial[:, at] = jnp.dot(w2_ref[...], hidden, preferred_element_type=f32)
        return 0

    lax.fori_loop(0, chunks, network, 0)

    cot = jnp.broadcast_to(cot_ref[...], (8, probes))

    def channel_tile(t, dens):
        c0 = pl.multiple_of(t * 8, 8)

        def forward(j, acc):
            at = pl.ds(pl.multiple_of(j * probes, probes), probes)
            scaled = feat[pl.ds(c0, 8), at]
            acc = list(acc)
            for l in range(degrees):
                message = radial[pl.ds(l * channels + c0, 8), at] * scaled
                for k in range(l * l, (l + 1) * (l + 1)):
                    acc[k] = acc[k] + (message if k == 0 else sphb[j, k] * message)
            return tuple(acc)

        zero = jnp.zeros((8, probes), f32)
        moment = lax.fori_loop(0, slots, forward, (zero,) * rows_k, unroll=4)
        grad = []
        for l in range(degrees):
            column = jnp.broadcast_to(readt_ref[pl.ds(c0, 8), l : l + 1], (8, probes))
            if l == 0:
                squared = moment[0]
                grad.append(cot * column)
            else:
                squared = moment[l * l] * moment[l * l]
                for k in range(l * l + 1, (l + 1) * (l + 1)):
                    squared = squared + moment[k] * moment[k]
                factor = 2.0 * cot * column
                for k in range(l * l, (l + 1) * (l + 1)):
                    grad.append(factor * moment[k])
            squares[l, pl.ds(c0, 8), :] = squared
            dens = dens + column * squared

        def backward(j, carry):
            at = pl.ds(pl.multiple_of(j * probes, probes), probes)
            scaled = feat[pl.ds(c0, 8), at]
            total_feat = None
            for l in range(degrees):
                message = None
                for k in range(l * l, (l + 1) * (l + 1)):
                    term = grad[k] if k == 0 else sphb[j, k] * grad[k]
                    message = term if message is None else message + term
                here = pl.ds(l * channels + c0, 8)
                term = message * radial[here, at]
                total_feat = term if total_feat is None else total_feat + term
                gradial[here, at] = message * scaled
            gfeat[pl.ds(c0, 8), at] = total_feat * sphb[j, rows_k]
            return carry

        lax.fori_loop(0, slots, backward, 0, unroll=4)
        return dens

    dens = lax.fori_loop(0, channels // 8, channel_tile, jnp.zeros((8, probes), f32))
    dens_ref[...] = jnp.sum(dens, axis=0, keepdims=True)

    gwin_acc[...] = jnp.zeros_like(gwin_acc)
    gw2_acc[...] = jnp.zeros_like(gw2_acc)
    gw1_acc[...] = jnp.zeros_like(gw1_acc)

    def weights(i, _):
        at = pl.ds(pl.multiple_of(i * chunk, chunk), chunk)
        grads = gradial[:, at].astype(bf16)
        gw2_acc[...] += lax.dot_general(grads, hid[:, at], NT, preferred_element_type=f32)
        ghid = lax.dot_general(w2_ref[...], grads, TN, preferred_element_type=f32)
        value = pre[:, at]
        logistic = jax.nn.sigmoid(value)
        gpre = ghid * logistic * (1.0 + value * (1.0 - logistic))
        gw1_acc[...] += lax.dot_general(
            basis[:, at], gpre, NT, precision=HIGH, preferred_element_type=f32
        )
        gwin_acc[...] += lax.dot_general(
            gfeat[:, at].astype(bf16), onehot[:, at], NT, preferred_element_type=f32
        )
        return 0

    lax.fori_loop(0, chunks, weights, 0)

    for b in range(blocks):
        gwin_ref[b] = gwin_acc[:, b * atoms : (b + 1) * atoms].astype(bf16)
    half, hidden_units = gw2_acc.shape[0] // 2, gw2_acc.shape[1]
    lines = jnp.concatenate([gw2_acc[:half], gw2_acc[half:]], axis=1)
    small = []
    for l in range(degrees):
        small.append(
            lax.dot_general(cot, squares[l], NT, precision=HIGH, preferred_element_type=f32)[:1]
        )
    small.append(jnp.zeros((8 - degrees, channels), f32))
    first = jnp.concatenate(small, axis=0)
    second = jnp.concatenate(
        [gw1_acc[...], jnp.zeros((n_basis, channels - hidden_units), f32)], axis=1
    )
    pack_ref[0:half] = lines.astype(bf16)
    pack_ref[half : half + 16] = jnp.concatenate([first, second], axis=0).astype(bf16)
    rest = pack_ref.shape[0] - half - 16
    pack_ref[half + 16 :] = jnp.zeros((rest, channels), bf16)


def reduce_kernel(
    n_slab,
    n_plane,
    low,
    gwin_ref,
    pack_ref,
    gfeat_ref,
    out_ref,
    land,
    part_b,
    part_c,
    land_a,
    land_b,
    land_c,
    halo_send,
    halo_recv,
    a_send,
    a_recv,
    b_send,
    b_recv,
    c_send,
    c_recv,
):
    slab, plane, peers = halo_peers(n_slab, n_plane)
    group, high = low * n_plane, n_slab // low
    size = pack_ref.shape[0] // group
    slab_low, slab_high = lax.rem(slab, low), slab // low
    me = slab_low * n_plane + plane
    near = []
    for t in range(1, group):
        to = lax.rem(me + t, group)
        near.append((to, (slab - slab_low + to // n_plane, lax.rem(to, n_plane))))
    far = []
    for t in range(1, high):
        to = lax.rem(slab_high + t, high)
        far.append((to * low + slab_low, plane))
    barrier = pltpu.get_barrier_semaphore()
    everyone = [(p[2], p[3]) for p in peers] + [n[1] for n in near] + far
    for device in everyone:
        pl.semaphore_signal(barrier, inc=1, device_id=device, device_id_type=MESH)
    pl.semaphore_wait(barrier, len(everyone))

    def send(source, target, send_sem, recv_sem, device):
        copy = pltpu.make_async_remote_copy(
            src_ref=source,
            dst_ref=target,
            send_sem=send_sem,
            recv_sem=recv_sem,
            device_id=device,
            device_id_type=MESH,
        )
        copy.start()
        return copy

    first = []
    for t, (to, device) in enumerate(near):
        rows = pl.ds(pl.multiple_of(to * size, 16), size)
        first.append(send(pack_ref.at[rows], land_a.at[t], a_send.at[t], a_recv.at[t], device))
    halo = []
    for t, (d, _, to_slab, to_plane) in enumerate(peers):
        halo.append(
            send(
                gwin_ref.at[(d + 1) * n_plane + to_plane],
                land.at[(d + 1) * n_plane + plane],
                halo_send.at[t],
                halo_recv.at[t],
                (to_slab, to_plane),
            )
        )
    land[n_plane + plane] = gwin_ref[n_plane + plane]
    total = pack_ref[pl.ds(pl.multiple_of(me * size, 16), size)].astype(f32)
    for t, copy in enumerate(first):
        copy.wait_recv()
        total = total + land_a[t].astype(f32)
    part_b[...] = total
    land_b[slab_high] = total
    second = []
    for t, device in enumerate(far):
        second.append(
            send(part_b, land_b.at[slab_high], b_send.at[t], b_recv.at[t], device)
        )
    for copy in second:
        copy.wait_recv()
    total = land_b[0]
    for t in range(1, high):
        total = total + land_b[t]
    part_c[...] = total.astype(bf16)
    land_c[me] = total.astype(bf16)
    third = []
    for t, (_, device) in enumerate(near):
        third.append(send(part_c, land_c.at[me], c_send.at[t], c_recv.at[t], device))
    for copy in halo:
        copy.wait_recv()
    gfeat = land[0].astype(f32)
    for b in range(1, land.shape[0]):
        gfeat = gfeat + land[b].astype(f32)
    gfeat_ref[...] = gfeat
    for copy in third:
        copy.wait_recv()
    for b in range(group):
        out_ref[b * size : (b + 1) * size] = land_c[b].astype(f32)
    for copy in first + halo + second + third:
        copy.wait_send()


def shards(
    n_slab,
    n_plane,
    probe_pos,
    atom_pos,
    atom_feat,
    neighbours,
    valid,
    w_radial1,
    w_radial2,
    readout,
    cotangent,
):
    channels, atoms = atom_feat.shape
    slots, probes = neighbours.shape
    units, n_basis = w_radial1.shape
    degrees = readout.shape[0]
    out_rows = w_radial2.shape[0]
    half = out_rows // 2
    edges = slots * probes
    blocks = 3 * n_plane
    lines = -(-(channels + atom_pos.shape[0]) // 16) * 16
    peers = blocks - 1
    own = jnp.concatenate(
        [atom_feat, atom_pos, jnp.zeros((lines - channels - atom_pos.shape[0], atoms), bf16)], axis=0
    )
    window = pl.pallas_call(
        functools.partial(halo_kernel, n_slab, n_plane),
        out_shape=jax.ShapeDtypeStruct((blocks, lines, atoms), bf16),
        in_specs=[VMEM],
        out_specs=VMEM,
        scratch_shapes=[
            pltpu.VMEM((blocks, lines, atoms), bf16),
            pltpu.SemaphoreType.DMA((peers,)),
            pltpu.SemaphoreType.DMA((peers,)),
        ],
        compiler_params=pltpu.CompilerParams(collective_id=0, has_side_effects=True),
        name="halo",
    )(own)
    low = 4 if n_slab % 4 == 0 else 1
    group, high = low * n_plane, n_slab // low
    size = -(-(half + 16) // (16 * group)) * 16
    width = blocks * atoms
    kinds = degrees * degrees + 1
    density, gwin, pack = pl.pallas_call(
        functools.partial(edge_kernel, n_slab, n_plane),
        out_shape=(
            jax.ShapeDtypeStruct((1, probes), f32),
            jax.ShapeDtypeStruct((blocks, channels, atoms), bf16),
            jax.ShapeDtypeStruct((size * group, channels), bf16),
        ),
        in_specs=[VMEM] * 9,
        out_specs=(VMEM,) * 3,
        scratch_shapes=[
            pltpu.VMEM((lines, width), bf16),
            pltpu.VMEM((slots, probes), jnp.int32),
            pltpu.VMEM((slots, probes), f32),
            pltpu.VMEM((3, slots, probes), f32),
            pltpu.VMEM((width, edges), bf16),
            pltpu.VMEM((channels, edges), f32),
            pltpu.VMEM((channels, edges), f32),
            pltpu.VMEM((kinds, slots, probes), f32),
            pltpu.VMEM((slots, kinds, 8, probes), f32),
            pltpu.VMEM((slots, probes), f32),
            pltpu.VMEM((n_basis, edges), f32),
            pltpu.VMEM((units, edges), f32),
            pltpu.VMEM((units, edges), bf16),
            pltpu.VMEM((out_rows, edges), f32),
            pltpu.VMEM((out_rows, edges), f32),
            pltpu.VMEM((degrees, channels, probes), f32),
            pltpu.VMEM((channels, width), f32),
            pltpu.VMEM((out_rows, units), f32),
            pltpu.VMEM((n_basis, units), f32),
        ],
        compiler_params=pltpu.CompilerParams(vmem_limit_bytes=52 * 1024 * 1024),
        name="edges",
    )(
        window,
        neighbours,
        valid,
        probe_pos,
        cotangent.reshape(1, probes),
        w_radial1,
        w_radial2,
        readout,
        readout.T,
    )
    grad_feat, summed = pl.pallas_call(
        functools.partial(reduce_kernel, n_slab, n_plane, low),
        out_shape=(
            jax.ShapeDtypeStruct((channels, atoms), f32),
            jax.ShapeDtypeStruct((size * group, channels), f32),
        ),
        in_specs=[VMEM] * 2,
        out_specs=(VMEM,) * 2,
        scratch_shapes=[
            pltpu.VMEM((blocks, channels, atoms), bf16),
            pltpu.VMEM((size, channels), f32),
            pltpu.VMEM((size, channels), bf16),
            pltpu.VMEM((group - 1, size, channels), bf16),
            pltpu.VMEM((high, size, channels), f32),
            pltpu.VMEM((group, size, channels), bf16),
            pltpu.SemaphoreType.DMA((peers,)),
            pltpu.SemaphoreType.DMA((peers,)),
            pltpu.SemaphoreType.DMA((group - 1,)),
            pltpu.SemaphoreType.DMA((group - 1,)),
            pltpu.SemaphoreType.DMA((high,)),
            pltpu.SemaphoreType.DMA((high,)),
            pltpu.SemaphoreType.DMA((group - 1,)),
            pltpu.SemaphoreType.DMA((group - 1,)),
        ],
        compiler_params=pltpu.CompilerParams(collective_id=1, has_side_effects=True),
        name="reduce",
    )(gwin, pack)
    scale = 1.0 / math.sqrt(probes * n_slab * n_plane)
    grad_w2 = jnp.concatenate([summed[:half, :units], summed[:half, units:]], axis=0) * scale
    grad_read = summed[half : half + degrees] * scale
    grad_w1 = summed[half + 8 : half + 8 + n_basis, :units].T * scale
    return density.reshape(-1), grad_feat, grad_w1, grad_w2, grad_read


def solution(mesh):
    both = P(None, ("slab", "plane"))
    in_specs = (both,) * 5 + (P(), P(), P(), P(("slab", "plane")))
    out_specs = (P(("slab", "plane")), both, P(), P(), P())
    body = functools.partial(shards, mesh.shape["slab"], mesh.shape["plane"])
    return jax.shard_map(
        body, mesh=mesh, in_specs=in_specs, out_specs=out_specs, check_vma=False
    )
```

time: 379 us -> 69.5 us (0.18)
  the two profiles are of different devices: /device:TPU:8 before, /device:TPU:0 now
where the time goes in v1:
time: 69.5 us; the launch traced here: 69.1 us
  Pallas kernels  58.4 us (84%)
  local copies, waits for them, and re-layouts  5.87 us (8%)
  other arithmetic  4.04 us (6%)
  between operations  0.78 us (1%)
    pallas_call x1, Pallas kernels, shards(): pl.pallas_call(functools.partial(edge_kernel, n_slab, n_plane), out_shape...  31.7 us
    pallas_call x1, Pallas kernels, shards(): pl.pallas_call(functools.partial(reduce_kernel, n_slab, n_plane, low), ou...  15.8 us
    pallas_call x1, Pallas kernels, shards(): pl.pallas_call(functools.partial(halo_kernel, n_slab, n_plane), out_shape...  10.9 us
    unnamed x29, local copies, waits for them, and re-layouts  4.7 us
    concatenate x1, other arithmetic, shards(): jnp.concatenate([atom_feat, atom_pos, jnp.zeros((lines - channels - atom_...  1.47 us

profile of v1, /device:TPU:0, one launch (start us, length us, event | category | flops | bytes accessed | tf_op | source)
XLA Modules:
  0.0 69.1 jit_solution(5905793044358500121)
XLA Ops:
  0.6 0.0 copy-start.10
  0.7 0.0 copy-start.11
  0.7 0.1 pad.4.clone
  0.7 0.6 copy-done.10
  1.3 0.1 copy.15.w1_ref
  1.4 1.5 %maximum_maximum_fusion.own_ref = bf16[144,128]{1,0:T(8,128)(2,1)} fusion(bf16[3,128]{1,0:T(4,128)(2,1)S(1)} %copy-done.11, bf16[128,128]{1,0:T(8,128)(2,1)} %param.11, bf16[144]{0:T(256)(128)(2,1)S(1)} %pad.4.clone), kind=kLoop, calls=%fused_computation.1 | loop fusion | flops 110592 | bytes 70688 | tf_op jit(solution)/shard_map/concatenate | solution.py:429
  2.9 0.1 copy.14
  3.0 0.0 copy-done.8
  3.0 0.2 copy.16.w2_ref
  3.2 0.0 copy-start.5
  3.2 0.0 copy-start.6
  3.2 0.0 copy-start.7
  3.2 10.9 %halo.1.win_ref = bf16[6,144,128]{2,1,0:T(8,128)(2,1)} custom-call(bf16[144,128]{1,0:T(8,128)(2,1)} %maximum_maximum_fusion.own_ref), custom_call_target="tpu_custom_call" | custom-call | tf_op jit(solution)/shard_map/halo/pallas_call | solution.py:432
  14.2 0.9 %copy-done = bf16[6,144,128]{2,1,0:T(8,128)(2,1)S(1)} copy-done((bf16[6,144,128]{2,1,0:T(8,128)(2,1)S(1)}, bf16[6,144,128]{2,1,0:T(8,128)(2,1)}, u32[]{:S(2)}) %copy-start) | copy-done | bytes 221208
  15.1 31.7 %edges.1 = (f32[1,128]{1,0:T(1,128)}, bf16[6,128,128]{2,1,0:T(8,128)(2,1)S(1)}, bf16[384,128]{1,0:T(8,128)(2,1)S(1)}) custom-call(bf16[6,144,128]{2,1,0:T(8,128)(2,1)S(1)} %copy-done, s32[32,128]{1,0:T(8,128)S(1)} %copy-done.4, s32[32,128]{1,0:T(8,128)S(1)} %copy-done.5, bf16[3,128]{1,0:T(4,128)(2,1)S(1)} %copy-done.6, f32[1,128]{1,0:T(1,128)S(1)} %bitcast.6, ...), custom_call_target="tpu_custom_call" | custom-call | tf_op jit(solution)/shard_map/edges/pallas_call | solution.py:450
  46.8 0.7 copy-done.1
  47.5 0.6 copy-done.2
  48.1 15.8 %reduce.1 = (f32[128,128]{1,0:T(8,128)}, f32[384,128]{1,0:T(8,128)}) custom-call(bf16[6,128,128]{2,1,0:T(8,128)(2,1)} %copy-done.1, bf16[384,128]{1,0:T(8,128)(2,1)} %copy-done.2), custom_call_target="tpu_custom_call" | custom-call | tf_op jit(solution)/shard_map/reduce/pallas_call | solution.py:493
  64.0 1.3 %slice_multiply_fusion = f32[5,128]{1,0:T(8,128)} fusion(f32[384,128]{1,0:T(8,128)} %get-tuple-element.14), kind=kLoop, calls=%fused_computation.2 | loop fusion | flops 640 | bytes 5120 | tf_op jit(solution)/shard_map/mul | solution.py:522
  65.2 1.3 %multiply_bitcast_fusion = f32[64,8]{0,1:T(8,128)} fusion(f32[384,128]{1,0:T(8,128)} %get-tuple-element.14), kind=kLoop, calls=%fused_computation.3 | loop fusion | flops 512 | bytes 4096 | tf_op jit(solution)/shard_map/mul | solution.py:523
  66.5 1.1 %fusion = (f32[320,64]{1,0:T(8,128)S(1)}, f32[320,64]{1,0:T(8,128)S(1)}) fusion(f32[384,128]{1,0:T(8,128)} %get-tuple-element.14), kind=kLoop, calls=%fused_computation.4 | loop fusion | bytes 327680 | tf_op jit(solution)/shard_map/slice | solution.py:521
  67.7 0.8 %copy.17 = f32[640,64]{0,1:T(8,128)} copy(f32[640,64]{1,0:T(8,128)S(1)} %maximum_multiply_fusion) | data formatting | bytes 327680
  68.5 0.0 copy-done.9
  68.5 0.6 copy.19
  (15 shorter events, 0.1 us)
Async XLA Ops:
  0.6 0.7 copy-start.10
  0.7 0.8 %copy-start.11 = (bf16[3,128]{1,0:T(4,128)(2,1)S(1)}, bf16[3,128]{1,0:T(4,128)(2,1)}, u32[]{:S(2)}) copy-start(bf16[3,128]{1,0:T(4,128)(2,1)} %param.10) | copy-start | bytes 2308
  1.3 1.7 %copy-start.8 = (bf16[640,64]{0,1:T(8,128)(2,1)S(1)}, bf16[640,64]{0,1:T(8,128)(2,1)}, u32[]{:S(2)}) copy-start(bf16[640,64]{0,1:T(8,128)(2,1)} %param.15) | copy-start | bytes 245764
  1.4 1.5 %copy-start.3 = (f32[5,128]{1,0:T(8,128)S(1)}, f32[5,128]{1,0:T(8,128)}, u32[]{:S(2)}) copy-start(f32[5,128]{1,0:T(8,128)} %read_ref.1) | copy-start | bytes 7684
  3.2 11.0 %copy-start.4 = (s32[32,128]{1,0:T(8,128)S(1)}, s32[32,128]{1,0:T(8,128)}, u32[]{:S(2)}) copy-start(s32[32,128]{1,0:T(8,128)} %nbr_ref.1) | copy-start | bytes 49156
  3.2 11.0 %copy-start.5 = (s32[32,128]{1,0:T(8,128)S(1)}, s32[32,128]{1,0:T(8,128)}, u32[]{:S(2)}) copy-start(s32[32,128]{1,0:T(8,128)} %valid_ref.1) | copy-start | bytes 49156
  3.2 11.0 %copy-start.6 = (bf16[3,128]{1,0:T(4,128)(2,1)S(1)}, bf16[3,128]{1,0:T(4,128)(2,1)}, u32[]{:S(2)}) copy-start(bf16[3,128]{1,0:T(4,128)(2,1)} %probe_ref.1) | copy-start | bytes 2308
  3.2 11.0 %copy-start.7 = (f32[128]{0:T(128)S(1)}, f32[128]{0:T(128)}, u32[]{:S(2)}) copy-start(f32[128]{0:T(128)} %param.17) | copy-start | bytes 1540
  14.2 0.9 %copy-start = (bf16[6,144,128]{2,1,0:T(8,128)(2,1)S(1)}, bf16[6,144,128]{2,1,0:T(8,128)(2,1)}, u32[]{:S(2)}) copy-start(bf16[6,144,128]{2,1,0:T(8,128)(2,1)} %halo.1.win_ref) | copy-start | bytes 663556
  46.8 0.7 copy-start.1
  47.5 0.6 copy-start.2
  67.6 0.8 %copy-start.9 = (f32[128,128]{1,0:T(8,128)S(1)}, f32[128,128]{1,0:T(8,128)}, u32[]{:S(2)}) copy-start(f32[128,128]{1,0:T(8,128)} %get-tuple-element.28) | copy-start | bytes 196612

commit v2 on v1

--- a/solution.py
+++ b/solution.py
@@ -16,7 +16,6 @@
 HIGH = lax.Precision.HIGHEST
 VMEM = pl.BlockSpec(memory_space=pltpu.VMEM)
 NT = (((1,), (1,)), ((), ()))
-TN = (((0,), (0,)), ((), ()))
 
 
 def harmonics(x, y, z):
@@ -68,16 +67,22 @@
     return slab, plane, peers
 
 
-def halo_kernel(n_slab, n_plane, own_ref, out_ref, land, send_sem, recv_sem):
+def halo_kernel(n_slab, n_plane, feat_ref, pos_ref, out_ref, own, land, send_sem, recv_sem):
     slab, plane, peers = halo_peers(n_slab, n_plane)
     barrier = pltpu.get_barrier_semaphore()
     for _, _, to_slab, to_plane in peers:
         pl.semaphore_signal(barrier, inc=1, device_id=(to_slab, to_plane), device_id_type=MESH)
+    channels = feat_ref.shape[0]
+    rest = own.shape[0] - channels - pos_ref.shape[0]
+    own[0:channels] = feat_ref[...]
+    own[channels:] = jnp.concatenate(
+        [pos_ref[...].astype(f32), jnp.zeros((rest, own.shape[1]), f32)], axis=0
+    ).astype(bf16)
     pl.semaphore_wait(barrier, len(peers))
     copies = []
     for number, (d, _, to_slab, to_plane) in enumerate(peers):
         copy = pltpu.make_async_remote_copy(
-            src_ref=own_ref,
+            src_ref=own,
             dst_ref=land.at[(1 - d) * n_plane + plane],
             send_sem=send_sem.at[number],
             recv_sem=recv_sem.at[number],
@@ -86,7 +91,7 @@
         )
         copy.start()
         copies.append(copy)
-    land[n_plane + plane] = own_ref[...]
+    land[n_plane + plane] = own[...]
     for copy in copies:
         copy.wait()
     out_ref[...] = land[...]
@@ -100,10 +105,9 @@
     valid_ref,
     probe_ref,
     cot_ref,
-    w1_ref,
-    w2_ref,
+    w1t_ref,
+    w2t_ref,
     read_ref,
-    readt_ref,
     dens_ref,
     gwin_ref,
     pack_ref,
@@ -126,6 +130,9 @@
     gwin_acc,
     gw2_acc,
     gw1_acc,
+    readt,
+    w1,
+    w2,
 ):
     slots, probes = nbr_ref.shape
     blocks, _, atoms = win_ref.shape
@@ -147,23 +154,29 @@
     offset = jnp.where(local < atom_slab, -1.0, jnp.where(local < 2 * atom_slab, 0.0, 1.0))
     atom_iota = lax.broadcasted_iota(jnp.int32, (width, probes), 0)
 
-    def gather(i, _):
+    readt[...] = jnp.concatenate(
+        [read_ref[...], jnp.zeros((8 - degrees, channels), f32)], axis=0
+    ).T
+    n_basis, units = w1t_ref.shape
+    w1[...] = jnp.concatenate(
+        [w1t_ref[...], jnp.zeros((n_basis, channels - units), f32)], axis=1
+    ).T[:units]
+    w2[...] = w2t_ref[...].astype(f32).T.astype(bf16)
+
+    for i in range(chunks):
         for s in range(per):
-            row = rows_s[pl.ds(i * per + s, 1), :]
-            at = pl.multiple_of(i * chunk + s * probes, probes)
-            onehot[:, pl.ds(at, probes)] = (atom_iota == row).astype(f32).astype(bf16)
-        at = pl.multiple_of(i * chunk, chunk)
-        got = jnp.dot(win[...], onehot[:, pl.ds(at, chunk)], preferred_element_type=f32)
+            row = rows_s[i * per + s : i * per + s + 1, :]
+            at = i * chunk + s * probes
+            onehot[:, at : at + probes] = (atom_iota == row).astype(f32).astype(bf16)
+        here = slice(i * chunk, (i + 1) * chunk)
+        got = jnp.dot(win[...], onehot[:, here], preferred_element_type=f32)
         for s in range(per):
             j = i * per + s
             part = got[:, s * probes : (s + 1) * probes]
-            at = pl.multiple_of(i * chunk + s * probes, probes)
-            feat[:, pl.ds(at, probes)] = part[:channels] * wgt[pl.ds(j, 1), :]
+            at = i * chunk + s * probes
+            feat[:, at : at + probes] = part[:channels] * wgt[j : j + 1, :]
             for k in range(3):
-                xyz[k, pl.ds(j, 1), :] = part[channels + k : channels + k + 1]
-        return 0
-
-    lax.fori_loop(0, chunks, gather, 0)
+                xyz[k, j : j + 1, :] = part[channels + k : channels + k + 1]
 
     probe = probe_ref[...].astype(f32)
     dx = xyz[0] - probe[0:1]
@@ -175,31 +188,22 @@
         sph[k] = row
     rows_k = degrees * degrees
     sph[rows_k] = wgt[...]
-
-    n_basis = w1_ref.shape[1]
     centres = 0.75 * lax.broadcasted_iota(jnp.int32, (n_basis, probes), 0).astype(f32)
 
-    def spread(j, _):
-        for k in range(rows_k + 1):
-            sphb[j, k] = jnp.broadcast_to(sph[k, pl.ds(j, 1), :], (8, probes))
-        shift = rad_s[pl.ds(j, 1), :] - centres
-        basis[:, pl.ds(pl.multiple_of(j * probes, probes), probes)] = jnp.exp(
-            -2.0 * (shift * shift)
-        )
-        return 0
-
-    lax.fori_loop(0, slots, spread, 0)
-
-    def network(i, _):
-        at = pl.ds(pl.multiple_of(i * chunk, chunk), chunk)
-        value = jnp.dot(w1_ref[...], basis[:, at], precision=HIGH, preferred_element_type=f32)
+    for j in range(slots):
+        shift = rad_s[j : j + 1, :] - centres
+        basis[:, j * probes : (j + 1) * probes] = jnp.exp(-2.0 * (shift * shift))
+
+    for i in range(chunks):
+        at = slice(i * chunk, (i + 1) * chunk)
+        for j in range(i * per, (i + 1) * per):
+            for k in range(rows_k + 1):
+                sphb[j, k] = jnp.broadcast_to(sph[k, j : j + 1, :], (8, probes))
+        value = jnp.dot(w1[...], basis[:, at], precision=HIGH, preferred_element_type=f32)
         pre[:, at] = value
         hidden = (value * jax.nn.sigmoid(value)).astype(bf16)
         hid[:, at] = hidden
-        radial[:, at] = jnp.dot(w2_ref[...], hidden, preferred_element_type=f32)
-        return 0
-
-    lax.fori_loop(0, chunks, network, 0)
+        radial[:, at] = jnp.dot(w2[...], hidden, preferred_element_type=f32)
 
     cot = jnp.broadcast_to(cot_ref[...], (8, probes))
 
@@ -220,7 +224,7 @@
         moment = lax.fori_loop(0, slots, forward, (zero,) * rows_k, unroll=4)
         grad = []
         for l in range(degrees):
-            column = jnp.broadcast_to(readt_ref[pl.ds(c0, 8), l : l + 1], (8, probes))
+            column = jnp.broadcast_to(readt[pl.ds(c0, 8), l : l + 1], (8, probes))
             if l == 0:
                 squared = moment[0]
                 grad.append(cot * column)
@@ -260,11 +264,11 @@
     gw2_acc[...] = jnp.zeros_like(gw2_acc)
     gw1_acc[...] = jnp.zeros_like(gw1_acc)
 
-    def weights(i, _):
-        at = pl.ds(pl.multiple_of(i * chunk, chunk), chunk)
+    for i in range(chunks):
+        at = slice(i * chunk, (i + 1) * chunk)
         grads = gradial[:, at].astype(bf16)
-        gw2_acc[...] += lax.dot_general(grads, hid[:, at], NT, preferred_element_type=f32)
-        ghid = lax.dot_general(w2_ref[...], grads, TN, preferred_element_type=f32)
+        gw2_acc[...] += lax.dot_general(hid[:, at], grads, NT, preferred_element_type=f32)
+        ghid = jnp.dot(w2t_ref[...], grads, preferred_element_type=f32)
         value = pre[:, at]
         logistic = jax.nn.sigmoid(value)
         gpre = ghid * logistic * (1.0 + value * (1.0 - logistic))
@@ -274,14 +278,14 @@
         gwin_acc[...] += lax.dot_general(
             gfeat[:, at].astype(bf16), onehot[:, at], NT, preferred_element_type=f32
         )
-        return 0
-
-    lax.fori_loop(0, chunks, weights, 0)
 
     for b in range(blocks):
         gwin_ref[b] = gwin_acc[:, b * atoms : (b + 1) * atoms].astype(bf16)
-    half, hidden_units = gw2_acc.shape[0] // 2, gw2_acc.shape[1]
-    lines = jnp.concatenate([gw2_acc[:half], gw2_acc[half:]], axis=1)
+    for l in range(degrees):
+        pack_ref[l * units : (l + 1) * units] = gw2_acc[
+            :, l * channels : (l + 1) * channels
+        ].astype(bf16)
+    half = degrees * units
     small = []
     for l in range(degrees):
         small.append(
@@ -290,9 +294,8 @@
     small.append(jnp.zeros((8 - degrees, channels), f32))
     first = jnp.concatenate(small, axis=0)
     second = jnp.concatenate(
-        [gw1_acc[...], jnp.zeros((n_basis, channels - hidden_units), f32)], axis=1
+        [gw1_acc[...], jnp.zeros((n_basis, channels - units), f32)], axis=1
     )
-    pack_ref[0:half] = lines.astype(bf16)
     pack_ref[half : half + 16] = jnp.concatenate([first, second], axis=0).astype(bf16)
     rest = pack_ref.shape[0] - half - 16
     pack_ref[half + 16 :] = jnp.zeros((rest, channels), bf16)
@@ -302,10 +305,14 @@
     n_slab,
     n_plane,
     low,
+    scale,
     gwin_ref,
     pack_ref,
     gfeat_ref,
-    out_ref,
+    gw1_ref,
+    gw2_ref,
+    gread_ref,
+    full,
     land,
     part_b,
     part_c,
@@ -398,7 +405,14 @@
     for copy in third:
         copy.wait_recv()
     for b in range(group):
-        out_ref[b * size : (b + 1) * size] = land_c[b].astype(f32)
+        full[b * size : (b + 1) * size] = land_c[b].astype(f32) * scale
+    units, channels = gw2_ref.shape[0], gwin_ref.shape[1]
+    degrees = gw2_ref.shape[1] // channels
+    for l in range(degrees):
+        gw2_ref[:, l * channels : (l + 1) * channels] = full[l * units : (l + 1) * units]
+    half = degrees * units
+    gread_ref[...] = full[half : half + gread_ref.shape[0]]
+    gw1_ref[...] = full[half + 8 : half + 8 + gw1_ref.shape[0], 0:units]
     for copy in first + halo + second + third:
         copy.wait_send()
 
@@ -421,27 +435,25 @@
     units, n_basis = w_radial1.shape
     degrees = readout.shape[0]
     out_rows = w_radial2.shape[0]
-    half = out_rows // 2
+    half = degrees * units
     edges = slots * probes
     blocks = 3 * n_plane
     lines = -(-(channels + atom_pos.shape[0]) // 16) * 16
     peers = blocks - 1
-    own = jnp.concatenate(
-        [atom_feat, atom_pos, jnp.zeros((lines - channels - atom_pos.shape[0], atoms), bf16)], axis=0
-    )
     window = pl.pallas_call(
         functools.partial(halo_kernel, n_slab, n_plane),
         out_shape=jax.ShapeDtypeStruct((blocks, lines, atoms), bf16),
-        in_specs=[VMEM],
+        in_specs=[VMEM] * 2,
         out_specs=VMEM,
         scratch_shapes=[
+            pltpu.VMEM((lines, atoms), bf16),
             pltpu.VMEM((blocks, lines, atoms), bf16),
             pltpu.SemaphoreType.DMA((peers,)),
             pltpu.SemaphoreType.DMA((peers,)),
         ],
         compiler_params=pltpu.CompilerParams(collective_id=0, has_side_effects=True),
         name="halo",
-    )(own)
+    )(atom_feat, atom_pos)
     low = 4 if n_slab % 4 == 0 else 1
     group, high = low * n_plane, n_slab // low
     size = -(-(half + 16) // (16 * group)) * 16
@@ -454,7 +466,7 @@
             jax.ShapeDtypeStruct((blocks, channels, atoms), bf16),
             jax.ShapeDtypeStruct((size * group, channels), bf16),
         ),
-        in_specs=[VMEM] * 9,
+        in_specs=[VMEM] * 8,
         out_specs=(VMEM,) * 3,
         scratch_shapes=[
             pltpu.VMEM((lines, width), bf16),
@@ -474,10 +486,13 @@
             pltpu.VMEM((out_rows, edges), f32),
             pltpu.VMEM((degrees, channels, probes), f32),
             pltpu.VMEM((channels, width), f32),
-            pltpu.VMEM((out_rows, units), f32),
+            pltpu.VMEM((units, out_rows), f32),
             pltpu.VMEM((n_basis, units), f32),
+            pltpu.VMEM((channels, 8), f32),
+            pltpu.VMEM((units, n_basis), f32),
+            pltpu.VMEM((out_rows, units), bf16),
         ],
-        compiler_params=pltpu.CompilerParams(vmem_limit_bytes=52 * 1024 * 1024),
+        compiler_params=pltpu.CompilerParams(vmem_limit_bytes=44 * 1024 * 1024),
         name="edges",
     )(
         window,
@@ -485,20 +500,23 @@
         valid,
         probe_pos,
         cotangent.reshape(1, probes),
-        w_radial1,
-        w_radial2,
+        w_radial1.T,
+        w_radial2.T,
         readout,
-        readout.T,
     )
-    grad_feat, summed = pl.pallas_call(
-        functools.partial(reduce_kernel, n_slab, n_plane, low),
+    scale = 1.0 / math.sqrt(probes * n_slab * n_plane)
+    grad_feat, grad_w1, grad_w2, grad_read = pl.pallas_call(
+        functools.partial(reduce_kernel, n_slab, n_plane, low, scale),
         out_shape=(
             jax.ShapeDtypeStruct((channels, atoms), f32),
-            jax.ShapeDtypeStruct((size * group, channels), f32),
+            jax.ShapeDtypeStruct((n_basis, units), f32),
+            jax.ShapeDtypeStruct((units, out_rows), f32),
+            jax.ShapeDtypeStruct((degrees, channels), f32),
         ),
         in_specs=[VMEM] * 2,
-        out_specs=(VMEM,) * 2,
+        out_specs=(VMEM,) * 4,
         scratch_shapes=[
+            pltpu.VMEM((size * group, channels), f32),
             pltpu.VMEM((blocks, channels, atoms), bf16),
             pltpu.VMEM((size, channels), f32),
             pltpu.VMEM((size, channels), bf16),
@@ -517,11 +535,7 @@
         compiler_params=pltpu.CompilerParams(collective_id=1, has_side_effects=True),
         name="reduce",
     )(gwin, pack)
-    scale = 1.0 / math.sqrt(probes * n_slab * n_plane)
-    grad_w2 = jnp.concatenate([summed[:half, :units], summed[:half, units:]], axis=0) * scale
-    grad_read = summed[half : half + degrees] * scale
-    grad_w1 = summed[half + 8 : half + 8 + n_basis, :units].T * scale
-    return density.reshape(-1), grad_feat, grad_w1, grad_w2, grad_read
+    return density.reshape(-1), grad_feat, grad_w1.T, grad_w2.T, grad_read
 
 
 def solution(mesh):

time: 69.5 us -> 59.8 us (0.86)
  Pallas kernels: 58.4 us -> 52.2 us
  other arithmetic: 4.04 us -> 0 us
    pallas_call x1, Pallas kernels: 31.7 us -> 25.4 us  [shards(): pl.pallas_call(functools.partial(edge_kernel, n_slab, n_plane), out_shape...]
    mul x3 -> x0, other arithmetic: 2.58 us -> none  [the longest x1 1.28 us: shards(): grad_w1 = summed[half + 8:half + 8 + n_basis, :units].T * scale]
    unnamed x29 -> x28, local copies, waits for them, and re-layouts: 4.7 us -> 6.53 us
    concatenate x1 -> x0, other arithmetic: 1.47 us -> none  [shards(): jnp.concatenate([atom_feat, atom_pos, jnp.zeros((lines - channels - atom_...]
    slice x1 -> x0, local copies, waits for them, and re-layouts: 1.09 us -> none  [shards(): summed[:half, :units]]
where the time goes in v2:
time: 59.8 us; the launch traced here: 59.5 us
  Pallas kernels  52.2 us (87%)
  local copies, waits for them, and re-layouts  6.53 us (11%)
  between operations  0.78 us (1%)
    pallas_call x1, Pallas kernels, shards(): pl.pallas_call(functools.partial(edge_kernel, n_slab, n_plane), out_shape...  25.4 us
    pallas_call x1, Pallas kernels, shards(): pl.pallas_call(functools.partial(reduce_kernel, n_slab, n_plane, low, sca...  15.8 us
    pallas_call x1, Pallas kernels, shards(): pl.pallas_call(functools.partial(halo_kernel, n_slab, n_plane), out_shape...  11 us
    unnamed x28, local copies, waits for them, and re-layouts  6.53 us

profile of v2, /device:TPU:0, one launch (start us, length us, event | category | flops | bytes accessed | tf_op | source)
XLA Modules:
  0.0 59.5 jit_solution(13588699928936075665)
XLA Ops:
  0.6 0.0 copy-start.3
  0.6 0.0 copy-start.4
  0.7 0.0 copy-start.5
  0.7 0.0 copy-start.6
  0.7 0.0 copy-start.7
  0.7 0.0 copy-start.8
  0.7 0.0 copy-start.9
  0.7 11.0 %halo.1.win_ref = bf16[6,144,128]{2,1,0:T(8,128)(2,1)} custom-call(bf16[128,128]{1,0:T(8,128)(2,1)} %feat_ref.1, bf16[3,128]{1,0:T(4,128)(2,1)} %pos_ref.1), custom_call_target="tpu_custom_call" | custom-call | tf_op jit(solution)/shard_map/halo/pallas_call | solution.py:443
  11.7 0.0 copy-done.3
  11.7 0.0 copy-done.4
  11.7 0.0 copy-done.5
  11.7 0.0 copy-done.6
  11.7 0.0 copy-done.7
  11.7 0.0 copy-done.8
  11.7 0.9 %copy-done = bf16[6,144,128]{2,1,0:T(8,128)(2,1)S(1)} copy-done((bf16[6,144,128]{2,1,0:T(8,128)(2,1)S(1)}, bf16[6,144,128]{2,1,0:T(8,128)(2,1)}, u32[]{:S(2)}) %copy-start) | copy-done | bytes 221208
  12.7 25.4 %edges.1 = (f32[1,128]{1,0:T(1,128)}, bf16[6,128,128]{2,1,0:T(8,128)(2,1)S(1)}, bf16[384,128]{1,0:T(8,128)(2,1)S(1)}) custom-call(bf16[6,144,128]{2,1,0:T(8,128)(2,1)S(1)} %copy-done, s32[32,128]{1,0:T(8,128)S(1)} %copy-done.4, s32[32,128]{1,0:T(8,128)S(1)} %copy-done.5, bf16[3,128]{1,0:T(4,128)(2,1)S(1)} %copy-done.8, f32[1,128]{1,0:T(1,128)S(1)} %bitcast.8, ...), custom_call_target="tpu_custom_call" | custom-call | tf_op jit(solution)/shard_map/edges/pallas_call | solution.py:462
  38.1 0.7 %copy-done.1 = bf16[6,128,128]{2,1,0:T(8,128)(2,1)} copy-done((bf16[6,128,128]{2,1,0:T(8,128)(2,1)}, bf16[6,128,128]{2,1,0:T(8,128)(2,1)S(1)}, u32[]{:S(2)}) %copy-start.1) | copy-done | bytes 196632
  38.8 0.6 %copy-done.2 = bf16[384,128]{1,0:T(8,128)(2,1)} copy-done((bf16[384,128]{1,0:T(8,128)(2,1)}, bf16[384,128]{1,0:T(8,128)(2,1)S(1)}, u32[]{:S(2)}) %copy-start.2) | copy-done | bytes 98328
  39.4 15.8 %reduce.1 = (f32[128,128]{1,0:T(8,128)}, f32[8,64]{1,0:T(8,128)}, f32[64,640]{1,0:T(8,128)}, f32[5,128]{1,0:T(8,128)}) custom-call(bf16[6,128,128]{2,1,0:T(8,128)(2,1)} %copy-done.1, bf16[384,128]{1,0:T(8,128)(2,1)} %copy-done.2), custom_call_target="tpu_custom_call" | custom-call | tf_op jit(solution)/shard_map/reduce/pallas_call | solution.py:508
  55.3 0.0 copy-start.11
  55.3 1.5 %copy.18 = f32[128,128]{1,0:T(8,128)} copy(f32[128,128]{1,0:T(8,128)} %get-tuple-element.25) | data formatting | bytes 131072
  56.8 0.6 copy.19
  57.3 1.6 %copy.20 = f32[640,64]{0,1:T(8,128)} copy(f32[640,64]{0,1:T(8,128)} %bitcast.9) | data formatting | bytes 327680
  58.9 0.6 copy.21
  (7 shorter events, 0.0 us)
Async XLA Ops:
  0.6 11.0 %copy-start.3 = (bf16[640,64]{0,1:T(8,128)(2,1)S(1)}, bf16[640,64]{0,1:T(8,128)(2,1)}, u32[]{:S(2)}) copy-start(bf16[640,64]{0,1:T(8,128)(2,1)} %param.15) | copy-start | bytes 245764
  0.6 11.0 %copy-start.4 = (s32[32,128]{1,0:T(8,128)S(1)}, s32[32,128]{1,0:T(8,128)}, u32[]{:S(2)}) copy-start(s32[32,128]{1,0:T(8,128)} %nbr_ref.1) | copy-start | bytes 49156
  0.7 11.0 %copy-start.5 = (s32[32,128]{1,0:T(8,128)S(1)}, s32[32,128]{1,0:T(8,128)}, u32[]{:S(2)}) copy-start(s32[32,128]{1,0:T(8,128)} %valid_ref.1) | copy-start | bytes 49156
  0.7 11.0 %copy-start.6 = (f32[64,8]{0,1:T(8,128)S(1)}, f32[64,8]{0,1:T(8,128)}, u32[]{:S(2)}) copy-start(f32[64,8]{0,1:T(8,128)} %param.14) | copy-start | bytes 6148
  0.7 11.0 %copy-start.7 = (f32[5,128]{1,0:T(8,128)S(1)}, f32[5,128]{1,0:T(8,128)}, u32[]{:S(2)}) copy-start(f32[5,128]{1,0:T(8,128)} %read_ref.1) | copy-start | bytes 7684
  0.7 11.0 %copy-start.8 = (bf16[3,128]{1,0:T(4,128)(2,1)S(1)}, bf16[3,128]{1,0:T(4,128)(2,1)}, u32[]{:S(2)}) copy-start(bf16[3,128]{1,0:T(4,128)(2,1)} %probe_ref.1) | copy-start | bytes 2308
  0.7 11.0 %copy-start.9 = (f32[128]{0:T(128)S(1)}, f32[128]{0:T(128)}, u32[]{:S(2)}) copy-start(f32[128]{0:T(128)} %param.17) | copy-start | bytes 1540
  11.7 0.9 %copy-start = (bf16[6,144,128]{2,1,0:T(8,128)(2,1)S(1)}, bf16[6,144,128]{2,1,0:T(8,128)(2,1)}, u32[]{:S(2)}) copy-start(bf16[6,144,128]{2,1,0:T(8,128)(2,1)} %halo.1.win_ref) | copy-start | bytes 663556
  38.1 0.7 %copy-start.1 = (bf16[6,128,128]{2,1,0:T(8,128)(2,1)}, bf16[6,128,128]{2,1,0:T(8,128)(2,1)S(1)}, u32[]{:S(2)}) copy-start(bf16[6,128,128]{2,1,0:T(8,128)(2,1)S(1)} %get-tuple-element.13.gwin_ref) | copy-start | bytes 589828
  38.8 0.6 %copy-start.2 = (bf16[384,128]{1,0:T(8,128)(2,1)}, bf16[384,128]{1,0:T(8,128)(2,1)S(1)}, u32[]{:S(2)}) copy-start(bf16[384,128]{1,0:T(8,128)(2,1)S(1)} %get-tuple-element.14.pack_ref) | copy-start | bytes 294916
  55.3 1.5 %copy-start.11 = (f32[8,64]{1,0:T(8,128)S(1)}, f32[8,64]{1,0:T(8,128)}, u32[]{:S(2)}) copy-start(f32[8,64]{1,0:T(8,128)} %get-tuple-element.16) | copy-start | bytes 6148
  57.3 1.6 %copy-start.10 = (f32[5,128]{1,0:T(8,128)S(1)}, f32[5,128]{1,0:T(8,128)}, u32[]{:S(2)}) copy-start(f32[5,128]{1,0:T(8,128)} %get-tuple-element.28) | copy-start | bytes 7684

commit v3 on v2

--- a/solution.py
+++ b/solution.py
@@ -15,6 +15,7 @@
 MESH = pl.DeviceIdType.MESH
 HIGH = lax.Precision.HIGHEST
 VMEM = pl.BlockSpec(memory_space=pltpu.VMEM)
+ANY = pl.BlockSpec(memory_space=pl.ANY)
 NT = (((1,), (1,)), ((), ()))
 
 
@@ -211,17 +212,19 @@
         c0 = pl.multiple_of(t * 8, 8)
 
         def forward(j, acc):
-            at = pl.ds(pl.multiple_of(j * probes, probes), probes)
+            at = slice(j * probes, (j + 1) * probes)
             scaled = feat[pl.ds(c0, 8), at]
             acc = list(acc)
             for l in range(degrees):
                 message = radial[pl.ds(l * channels + c0, 8), at] * scaled
                 for k in range(l * l, (l + 1) * (l + 1)):
                     acc[k] = acc[k] + (message if k == 0 else sphb[j, k] * message)
-            return tuple(acc)
+            return acc
 
         zero = jnp.zeros((8, probes), f32)
-        moment = lax.fori_loop(0, slots, forward, (zero,) * rows_k, unroll=4)
+        moment = [zero] * rows_k
+        for j in range(slots):
+            moment = forward(j, moment)
         grad = []
         for l in range(degrees):
             column = jnp.broadcast_to(readt[pl.ds(c0, 8), l : l + 1], (8, probes))
@@ -238,8 +241,8 @@
             squares[l, pl.ds(c0, 8), :] = squared
             dens = dens + column * squared
 
-        def backward(j, carry):
-            at = pl.ds(pl.multiple_of(j * probes, probes), probes)
+        for j in range(slots):
+            at = slice(j * probes, (j + 1) * probes)
             scaled = feat[pl.ds(c0, 8), at]
             total_feat = None
             for l in range(degrees):
@@ -252,9 +255,6 @@
                 total_feat = term if total_feat is None else total_feat + term
                 gradial[here, at] = message * scaled
             gfeat[pl.ds(c0, 8), at] = total_feat * sphb[j, rows_k]
-            return carry
-
-        lax.fori_loop(0, slots, backward, 0, unroll=4)
         return dens
 
     dens = lax.fori_loop(0, channels // 8, channel_tile, jnp.zeros((8, probes), f32))
@@ -305,14 +305,11 @@
     n_slab,
     n_plane,
     low,
-    scale,
     gwin_ref,
     pack_ref,
     gfeat_ref,
-    gw1_ref,
-    gw2_ref,
-    gread_ref,
-    full,
+    out_ref,
+    mine,
     land,
     part_b,
     part_c,
@@ -327,6 +324,7 @@
     b_recv,
     c_send,
     c_recv,
+    own_sem,
 ):
     slab, plane, peers = halo_peers(n_slab, n_plane)
     group, high = low * n_plane, n_slab // low
@@ -341,6 +339,12 @@
     for t in range(1, high):
         to = lax.rem(slab_high + t, high)
         far.append((to * low + slab_low, plane))
+    own_rows = pl.ds(pl.multiple_of(me * size, 16), size)
+    own_pack = pltpu.make_async_copy(pack_ref.at[own_rows], mine, own_sem.at[0])
+    own_pack.start()
+    own_block = n_plane + plane
+    own_gwin = pltpu.make_async_copy(gwin_ref.at[own_block], land.at[own_block], own_sem.at[1])
+    own_gwin.start()
     barrier = pltpu.get_barrier_semaphore()
     everyone = [(p[2], p[3]) for p in peers] + [n[1] for n in near] + far
     for device in everyone:
@@ -374,8 +378,9 @@
                 (to_slab, to_plane),
             )
         )
-    land[n_plane + plane] = gwin_ref[n_plane + plane]
-    total = pack_ref[pl.ds(pl.multiple_of(me * size, 16), size)].astype(f32)
+    own_pack.wait()
+    own_gwin.wait()
+    total = mine[...].astype(f32)
     for t, copy in enumerate(first):
         copy.wait_recv()
         total = total + land_a[t].astype(f32)
@@ -405,16 +410,31 @@
     for copy in third:
         copy.wait_recv()
     for b in range(group):
-        full[b * size : (b + 1) * size] = land_c[b].astype(f32) * scale
-    units, channels = gw2_ref.shape[0], gwin_ref.shape[1]
+        out_ref[b * size : (b + 1) * size] = land_c[b]
+    for copy in first + halo + second + third:
+        copy.wait_send()
+
+
+def finish_kernel(
+    scale, feat_ref, pack_ref, gfeat_ref, gw1_ref, gw2_ref, gread_ref, full, sems
+):
+    copies = [
+        pltpu.make_async_copy(pack_ref, full, sems.at[0]),
+        pltpu.make_async_copy(feat_ref, gfeat_ref, sems.at[1]),
+    ]
+    for copy in copies:
+        copy.start()
+    copies[0].wait()
+    units, channels = gw2_ref.shape[0], full.shape[1]
     degrees = gw2_ref.shape[1] // channels
     for l in range(degrees):
-        gw2_ref[:, l * channels : (l + 1) * channels] = full[l * units : (l + 1) * units]
+        rows = full[l * units : (l + 1) * units].astype(f32)
+        gw2_ref[:, l * channels : (l + 1) * channels] = rows * scale
     half = degrees * units
-    gread_ref[...] = full[half : half + gread_ref.shape[0]]
-    gw1_ref[...] = full[half + 8 : half + 8 + gw1_ref.shape[0], 0:units]
-    for copy in first + halo + second + third:
-        copy.wait_send()
+    rows = full[half : half + 16].astype(f32) * scale
+    gread_ref[...] = rows[: gread_ref.shape[0]]
+    gw1_ref[...] = rows[8 : 8 + gw1_ref.shape[0], :units]
+    copies[1].wait()
 
 
 def shards(
@@ -504,19 +524,16 @@
         w_radial2.T,
         readout,
     )
-    scale = 1.0 / math.sqrt(probes * n_slab * n_plane)
-    grad_feat, grad_w1, grad_w2, grad_read = pl.pallas_call(
-        functools.partial(reduce_kernel, n_slab, n_plane, low, scale),
+    feat_sum, pack_sum = pl.pallas_call(
+        functools.partial(reduce_kernel, n_slab, n_plane, low),
         out_shape=(
             jax.ShapeDtypeStruct((channels, atoms), f32),
-            jax.ShapeDtypeStruct((n_basis, units), f32),
-            jax.ShapeDtypeStruct((units, out_rows), f32),
-            jax.ShapeDtypeStruct((degrees, channels), f32),
+            jax.ShapeDtypeStruct((size * group, channels), bf16),
         ),
-        in_specs=[VMEM] * 2,
-        out_specs=(VMEM,) * 4,
+        in_specs=[ANY] * 2,
+        out_specs=(VMEM,) * 2,
         scratch_shapes=[
-            pltpu.VMEM((size * group, channels), f32),
+            pltpu.VMEM((size, channels), bf16),
             pltpu.VMEM((blocks, channels, atoms), bf16),
             pltpu.VMEM((size, channels), f32),
             pltpu.VMEM((size, channels), bf16),
@@ -531,10 +548,28 @@
             pltpu.SemaphoreType.DMA((high,)),
             pltpu.SemaphoreType.DMA((group - 1,)),
             pltpu.SemaphoreType.DMA((group - 1,)),
+            pltpu.SemaphoreType.DMA((2,)),
         ],
         compiler_params=pltpu.CompilerParams(collective_id=1, has_side_effects=True),
         name="reduce",
     )(gwin, pack)
+    scale = 1.0 / math.sqrt(probes * n_slab * n_plane)
+    grad_feat, grad_w1, grad_w2, grad_read = pl.pallas_call(
+        functools.partial(finish_kernel, scale),
+        out_shape=(
+            jax.ShapeDtypeStruct((channels, atoms), f32),
+            jax.ShapeDtypeStruct((n_basis, units), f32),
+            jax.ShapeDtypeStruct((units, out_rows), f32),
+            jax.ShapeDtypeStruct((degrees, channels), f32),
+        ),
+        in_specs=[ANY] * 2,
+        out_specs=(VMEM,) * 4,
+        scratch_shapes=[
+            pltpu.VMEM((size * group, channels), bf16),
+            pltpu.SemaphoreType.DMA((2,)),
+        ],
+        name="finish",
+    )(feat_sum, pack_sum)
     return density.reshape(-1), grad_feat, grad_w1.T, grad_w2.T, grad_read
 
 

time: 59.8 us -> 53.3 us (0.89)
  local copies, waits for them, and re-layouts: 6.53 us -> 2.27 us
  Pallas kernels: 52.2 us -> 50.1 us
    unnamed x28 -> x20, local copies, waits for them, and re-layouts: 6.53 us -> 2.27 us
    pallas_call x1, Pallas kernels: 25.4 us -> 22.5 us  [shards(): pl.pallas_call(functools.partial(edge_kernel, n_slab, n_plane), out_shape...]
    pallas_call x1 -> x2, Pallas kernels: 15.8 us -> 16.6 us  [the longest x1 15 us: shards(): pl.pallas_call(functools.partial(reduce_kernel, n_slab, n_plane, low), ou...]
where the time goes in v3:
time: 53.3 us; the launch traced here: 53.1 us
  Pallas kernels  50.1 us (94%)
  local copies, waits for them, and re-layouts  2.27 us (4%)
  between operations  0.77 us (1%)
    pallas_call x1, Pallas kernels, shards(): pl.pallas_call(functools.partial(edge_kernel, n_slab, n_plane), out_shape...  22.5 us
    pallas_call x1, Pallas kernels, shards(): pl.pallas_call(functools.partial(reduce_kernel, n_slab, n_plane, low), ou...  15 us
    pallas_call x1, Pallas kernels, shards(): pl.pallas_call(functools.partial(halo_kernel, n_slab, n_plane), out_shape...  11 us
    unnamed x20, local copies, waits for them, and re-layouts  2.27 us
    pallas_call x1, Pallas kernels, shards(): pl.pallas_call(functools.partial(finish_kernel, scale), out_shape=(jax.Sh...  1.62 us

profile of v3, /device:TPU:0, one launch (start us, length us, event | category | flops | bytes accessed | tf_op | source)
XLA Modules:
  0.0 53.1 jit_solution(9590175855985643144)
XLA Ops:
  0.6 0.0 copy-start.3
  0.6 0.0 copy-start.4
  0.7 0.0 copy-start.5
  0.7 0.0 copy-start.6
  0.7 0.0 copy-start.7
  0.7 0.0 copy-start.8
  0.7 0.0 copy-start.9
  0.7 11.0 %halo.1.win_ref = bf16[6,144,128]{2,1,0:T(8,128)(2,1)} custom-call(bf16[128,128]{1,0:T(8,128)(2,1)} %feat_ref.1, bf16[3,128]{1,0:T(4,128)(2,1)} %pos_ref.1), custom_call_target="tpu_custom_call" | custom-call | tf_op jit(solution)/shard_map/halo/pallas_call | solution.py:463
  11.7 0.0 copy-done.3
  11.7 0.0 copy-done.4
  11.7 0.0 copy-done.5
  11.7 0.0 copy-done.6
  11.7 0.0 copy-done.7
  11.7 0.0 copy-done.8
  11.7 0.0 copy-done.9
  11.7 0.0 copy-start
  11.8 0.9 %copy-done = bf16[6,144,128]{2,1,0:T(8,128)(2,1)S(1)} copy-done((bf16[6,144,128]{2,1,0:T(8,128)(2,1)S(1)}, bf16[6,144,128]{2,1,0:T(8,128)(2,1)}, u32[]{:S(2)}) %copy-start) | copy-done | bytes 221208
  12.7 22.5 %edges.1 = (f32[1,128]{1,0:T(1,128)}, bf16[6,128,128]{2,1,0:T(8,128)(2,1)S(1)}, bf16[384,128]{1,0:T(8,128)(2,1)S(1)}) custom-call(bf16[6,144,128]{2,1,0:T(8,128)(2,1)S(1)} %copy-done, s32[32,128]{1,0:T(8,128)S(1)} %copy-done.4, s32[32,128]{1,0:T(8,128)S(1)} %copy-done.5, bf16[3,128]{1,0:T(4,128)(2,1)S(1)} %copy-done.8, f32[1,128]{1,0:T(1,128)S(1)} %bitcast.8, ...), custom_call_target="tpu_custom_call" | custom-call | tf_op jit(solution)/shard_map/edges/pallas_call | solution.py:482
  35.2 0.0 copy-start.1
  35.2 0.7 %copy-done.1 = bf16[6,128,128]{2,1,0:T(8,128)(2,1)} copy-done((bf16[6,128,128]{2,1,0:T(8,128)(2,1)}, bf16[6,128,128]{2,1,0:T(8,128)(2,1)S(1)}, u32[]{:S(2)}) %copy-start.1) | copy-done | bytes 196632
  35.8 0.0 copy-start.2
  35.8 0.6 %copy-done.2 = bf16[384,128]{1,0:T(8,128)(2,1)} copy-done((bf16[384,128]{1,0:T(8,128)(2,1)}, bf16[384,128]{1,0:T(8,128)(2,1)S(1)}, u32[]{:S(2)}) %copy-start.2) | copy-done | bytes 98328
  36.5 15.0 %reduce.1 = (f32[128,128]{1,0:T(8,128)}, bf16[384,128]{1,0:T(8,128)(2,1)}) custom-call(bf16[6,128,128]{2,1,0:T(8,128)(2,1)} %copy-done.1, bf16[384,128]{1,0:T(8,128)(2,1)} %copy-done.2), custom_call_target="tpu_custom_call" | custom-call | tf_op jit(solution)/shard_map/reduce/pallas_call | solution.py:527
  51.5 1.6 %finish.1 = (f32[128,128]{1,0:T(8,128)}, f32[8,64]{1,0:T(8,128)}, f32[64,640]{1,0:T(8,128)}, f32[5,128]{1,0:T(8,128)}) custom-call(f32[128,128]{1,0:T(8,128)} %get-tuple-element.17.feat_ref, bf16[384,128]{1,0:T(8,128)(2,1)} %get-tuple-element.18.pack_ref), custom_call_target="tpu_custom_call" | custom-call | tf_op jit(solution)/shard_map/finish/pallas_call | solution.py:557
Async XLA Ops:
  0.6 11.0 %copy-start.3 = (bf16[640,64]{0,1:T(8,128)(2,1)S(1)}, bf16[640,64]{0,1:T(8,128)(2,1)}, u32[]{:S(2)}) copy-start(bf16[640,64]{0,1:T(8,128)(2,1)} %param.15) | copy-start | bytes 245764
  0.6 11.0 %copy-start.4 = (s32[32,128]{1,0:T(8,128)S(1)}, s32[32,128]{1,0:T(8,128)}, u32[]{:S(2)}) copy-start(s32[32,128]{1,0:T(8,128)} %nbr_ref.1) | copy-start | bytes 49156
  0.7 11.0 %copy-start.5 = (s32[32,128]{1,0:T(8,128)S(1)}, s32[32,128]{1,0:T(8,128)}, u32[]{:S(2)}) copy-start(s32[32,128]{1,0:T(8,128)} %valid_ref.1) | copy-start | bytes 49156
  0.7 11.0 %copy-start.6 = (f32[64,8]{0,1:T(8,128)S(1)}, f32[64,8]{0,1:T(8,128)}, u32[]{:S(2)}) copy-start(f32[64,8]{0,1:T(8,128)} %param.14) | copy-start | bytes 6148
  0.7 11.0 %copy-start.7 = (f32[5,128]{1,0:T(8,128)S(1)}, f32[5,128]{1,0:T(8,128)}, u32[]{:S(2)}) copy-start(f32[5,128]{1,0:T(8,128)} %read_ref.1) | copy-start | bytes 7684
  0.7 11.0 %copy-start.8 = (bf16[3,128]{1,0:T(4,128)(2,1)S(1)}, bf16[3,128]{1,0:T(4,128)(2,1)}, u32[]{:S(2)}) copy-start(bf16[3,128]{1,0:T(4,128)(2,1)} %probe_ref.1) | copy-start | bytes 2308
  0.7 11.0 %copy-start.9 = (f32[128]{0:T(128)S(1)}, f32[128]{0:T(128)}, u32[]{:S(2)}) copy-start(f32[128]{0:T(128)} %param.17) | copy-start | bytes 1540
  11.7 0.9 %copy-start = (bf16[6,144,128]{2,1,0:T(8,128)(2,1)S(1)}, bf16[6,144,128]{2,1,0:T(8,128)(2,1)}, u32[]{:S(2)}) copy-start(bf16[6,144,128]{2,1,0:T(8,128)(2,1)} %halo.1.win_ref) | copy-start | bytes 663556
  35.2 0.7 %copy-start.1 = (bf16[6,128,128]{2,1,0:T(8,128)(2,1)}, bf16[6,128,128]{2,1,0:T(8,128)(2,1)S(1)}, u32[]{:S(2)}) copy-start(bf16[6,128,128]{2,1,0:T(8,128)(2,1)S(1)} %get-tuple-element.15.gwin_ref) | copy-start | bytes 589828
  35.8 0.6 %copy-start.2 = (bf16[384,128]{1,0:T(8,128)(2,1)}, bf16[384,128]{1,0:T(8,128)(2,1)S(1)}, u32[]{:S(2)}) copy-start(bf16[384,128]{1,0:T(8,128)(2,1)S(1)} %get-tuple-element.16.pack_ref) | copy-start | bytes 294916

commit v4 on v3

--- a/solution.py
+++ b/solution.py
@@ -15,6 +15,7 @@
 MESH = pl.DeviceIdType.MESH
 HIGH = lax.Precision.HIGHEST
 VMEM = pl.BlockSpec(memory_space=pltpu.VMEM)
+HBM = pl.BlockSpec(memory_space=pltpu.HBM)
 ANY = pl.BlockSpec(memory_space=pl.ANY)
 NT = (((1,), (1,)), ((), ()))
 
@@ -208,56 +209,72 @@
 
     cot = jnp.broadcast_to(cot_ref[...], (8, probes))
 
-    def channel_tile(t, dens):
-        c0 = pl.multiple_of(t * 8, 8)
-
-        def forward(j, acc):
-            at = slice(j * probes, (j + 1) * probes)
-            scaled = feat[pl.ds(c0, 8), at]
-            acc = list(acc)
+    pair = range(2)
+    groups = (tuple(range(degrees - 1)), (degrees - 1,))
+
+    def orders(l):
+        return range(l * l, (l + 1) * (l + 1))
+
+    def channel_pair(t, dens):
+        starts = [pl.multiple_of(t * 16 + 8 * h, 8) for h in pair]
+        zero = jnp.zeros((8, probes), f32)
+        moment = [[zero] * rows_k for _ in pair]
+        for group in groups:
+            for j in range(slots):
+                at = slice(j * probes, (j + 1) * probes)
+                scaled = [feat[pl.ds(c, 8), at] for c in starts]
+                for l in group:
+                    message = [
+                        radial[pl.ds(l * channels + starts[h], 8), at] * scaled[h] for h in pair
+                    ]
+                    for k in orders(l):
+                        factor = None if k == 0 else sphb[j, k]
+                        for h in pair:
+                            term = message[h] if k == 0 else factor * message[h]
+                            moment[h][k] = moment[h][k] + term
+        grad = [[None] * rows_k for _ in pair]
+        for h in pair:
             for l in range(degrees):
-                message = radial[pl.ds(l * channels + c0, 8), at] * scaled
-                for k in range(l * l, (l + 1) * (l + 1)):
-                    acc[k] = acc[k] + (message if k == 0 else sphb[j, k] * message)
-            return acc
-
-        zero = jnp.zeros((8, probes), f32)
-        moment = [zero] * rows_k
-        for j in range(slots):
-            moment = forward(j, moment)
-        grad = []
-        for l in range(degrees):
-            column = jnp.broadcast_to(readt[pl.ds(c0, 8), l : l + 1], (8, probes))
-            if l == 0:
-                squared = moment[0]
-                grad.append(cot * column)
-            else:
-                squared = moment[l * l] * moment[l * l]
-                for k in range(l * l + 1, (l + 1) * (l + 1)):
-                    squared = squared + moment[k] * moment[k]
-                factor = 2.0 * cot * column
-                for k in range(l * l, (l + 1) * (l + 1)):
-                    grad.append(factor * moment[k])
-            squares[l, pl.ds(c0, 8), :] = squared
-            dens = dens + column * squared
-
-        for j in range(slots):
-            at = slice(j * probes, (j + 1) * probes)
-            scaled = feat[pl.ds(c0, 8), at]
-            total_feat = None
-            for l in range(degrees):
-                message = None
-                for k in range(l * l, (l + 1) * (l + 1)):
-                    term = grad[k] if k == 0 else sphb[j, k] * grad[k]
-                    message = term if message is None else message + term
-                here = pl.ds(l * channels + c0, 8)
-                term = message * radial[here, at]
-                total_feat = term if total_feat is None else total_feat + term
-                gradial[here, at] = message * scaled
-            gfeat[pl.ds(c0, 8), at] = total_feat * sphb[j, rows_k]
+                rows = pl.ds(starts[h], 8)
+                column = jnp.broadcast_to(readt[rows, l : l + 1], (8, probes))
+                if l == 0:
+                    squared = moment[h][0]
+                    grad[h][0] = cot * column
+                else:
+                    squared = None
+                    factor = 2.0 * cot * column
+                    for k in orders(l):
+                        term = moment[h][k] * moment[h][k]
+                        squared = term if squared is None else squared + term
+                        grad[h][k] = factor * moment[h][k]
+                squares[l, rows, :] = squared
+                dens = dens + column * squared
+        for number, group in enumerate(groups):
+            for j in range(slots):
+                at = slice(j * probes, (j + 1) * probes)
+                scaled = [feat[pl.ds(c, 8), at] for c in starts]
+                total = [None for _ in pair]
+                for l in group:
+                    message = [None for _ in pair]
+                    for k in orders(l):
+                        factor = None if k == 0 else sphb[j, k]
+                        for h in pair:
+                            term = grad[h][k] if k == 0 else factor * grad[h][k]
+                            message[h] = term if message[h] is None else message[h] + term
+                    for h in pair:
+                        here = pl.ds(l * channels + starts[h], 8)
+                        term = message[h] * radial[here, at]
+                        total[h] = term if total[h] is None else total[h] + term
+                        gradial[here, at] = message[h] * scaled[h]
+                for h in pair:
+                    rows = pl.ds(starts[h], 8)
+                    if number == 0:
+                        gfeat[rows, at] = total[h]
+                    else:
+                        gfeat[rows, at] = (gfeat[rows, at] + total[h]) * sphb[j, rows_k]
         return dens
 
-    dens = lax.fori_loop(0, channels // 8, channel_tile, jnp.zeros((8, probes), f32))
+    dens = lax.fori_loop(0, channels // 16, channel_pair, jnp.zeros((8, probes), f32))
     dens_ref[...] = jnp.sum(dens, axis=0, keepdims=True)
 
     gwin_acc[...] = jnp.zeros_like(gwin_acc)
@@ -530,7 +547,7 @@
             jax.ShapeDtypeStruct((channels, atoms), f32),
             jax.ShapeDtypeStruct((size * group, channels), bf16),
         ),
-        in_specs=[ANY] * 2,
+        in_specs=[HBM] * 2,
         out_specs=(VMEM,) * 2,
         scratch_shapes=[
             pltpu.VMEM((size, channels), bf16),

time: 53.3 us -> 53.7 us (level)
  no operation moved by 1% of the time
where the time goes in v4:
time: 53.7 us; the launch traced here: 53.5 us
  Pallas kernels  50.4 us (94%)
  local copies, waits for them, and re-layouts  2.27 us (4%)
  between operations  0.77 us (1%)
    pallas_call x1, Pallas kernels, shards(): pl.pallas_call(functools.partial(edge_kernel, n_slab, n_plane), out_shape...  22.8 us
    pallas_call x1, Pallas kernels, shards(): pl.pallas_call(functools.partial(reduce_kernel, n_slab, n_plane, low), ou...  15 us
    pallas_call x1, Pallas kernels, shards(): pl.pallas_call(functools.partial(halo_kernel, n_slab, n_plane), out_shape...  11 us
    unnamed x20, local copies, waits for them, and re-layouts  2.27 us
    pallas_call x1, Pallas kernels, shards(): pl.pallas_call(functools.partial(finish_kernel, scale), out_shape=(jax.Sh...  1.62 us

profile of v4, /device:TPU:0, one launch (start us, length us, event | category | flops | bytes accessed | tf_op | source)
XLA Modules:
  0.0 53.5 jit_solution(15163954340295394109)
XLA Ops:
  0.6 0.0 copy-start.3
  0.6 0.0 copy-start.4
  0.7 0.0 copy-start.5
  0.7 0.0 copy-start.6
  0.7 0.0 copy-start.7
  0.7 0.0 copy-start.8
  0.7 0.0 copy-start.9
  0.7 11.0 %halo.1.win_ref = bf16[6,144,128]{2,1,0:T(8,128)(2,1)} custom-call(bf16[128,128]{1,0:T(8,128)(2,1)} %feat_ref.1, bf16[3,128]{1,0:T(4,128)(2,1)} %pos_ref.1), custom_call_target="tpu_custom_call" | custom-call | tf_op jit(solution)/shard_map/halo/pallas_call | solution.py:480
  11.7 0.0 copy-done.3
  11.7 0.0 copy-done.4
  11.7 0.0 copy-done.5
  11.7 0.0 copy-done.6
  11.7 0.0 copy-done.7
  11.7 0.0 copy-done.8
  11.7 0.0 copy-done.9
  11.7 0.0 copy-start
  11.8 0.9 %copy-done = bf16[6,144,128]{2,1,0:T(8,128)(2,1)S(1)} copy-done((bf16[6,144,128]{2,1,0:T(8,128)(2,1)S(1)}, bf16[6,144,128]{2,1,0:T(8,128)(2,1)}, u32[]{:S(2)}) %copy-start) | copy-done | bytes 221208
  12.7 22.8 %edges.1 = (f32[1,128]{1,0:T(1,128)}, bf16[6,128,128]{2,1,0:T(8,128)(2,1)S(1)}, bf16[384,128]{1,0:T(8,128)(2,1)S(1)}) custom-call(bf16[6,144,128]{2,1,0:T(8,128)(2,1)S(1)} %copy-done, s32[32,128]{1,0:T(8,128)S(1)} %copy-done.4, s32[32,128]{1,0:T(8,128)S(1)} %copy-done.5, bf16[3,128]{1,0:T(4,128)(2,1)S(1)} %copy-done.8, f32[1,128]{1,0:T(1,128)S(1)} %bitcast.8, ...), custom_call_target="tpu_custom_call" | custom-call | tf_op jit(solution)/shard_map/edges/pallas_call | solution.py:499
  35.5 0.0 copy-start.1
  35.5 0.7 %copy-done.1 = bf16[6,128,128]{2,1,0:T(8,128)(2,1)} copy-done((bf16[6,128,128]{2,1,0:T(8,128)(2,1)}, bf16[6,128,128]{2,1,0:T(8,128)(2,1)S(1)}, u32[]{:S(2)}) %copy-start.1) | copy-done | bytes 196632
  36.2 0.0 copy-start.2
  36.2 0.6 %copy-done.2 = bf16[384,128]{1,0:T(8,128)(2,1)} copy-done((bf16[384,128]{1,0:T(8,128)(2,1)}, bf16[384,128]{1,0:T(8,128)(2,1)S(1)}, u32[]{:S(2)}) %copy-start.2) | copy-done | bytes 98328
  36.8 15.0 %reduce.1 = (f32[128,128]{1,0:T(8,128)}, bf16[384,128]{1,0:T(8,128)(2,1)}) custom-call(bf16[6,128,128]{2,1,0:T(8,128)(2,1)} %copy-done.1, bf16[384,128]{1,0:T(8,128)(2,1)} %copy-done.2), custom_call_target="tpu_custom_call" | custom-call | tf_op jit(solution)/shard_map/reduce/pallas_call | solution.py:544
  51.9 1.6 %finish.1 = (f32[128,128]{1,0:T(8,128)}, f32[8,64]{1,0:T(8,128)}, f32[64,640]{1,0:T(8,128)}, f32[5,128]{1,0:T(8,128)}) custom-call(f32[128,128]{1,0:T(8,128)} %get-tuple-element.17.feat_ref, bf16[384,128]{1,0:T(8,128)(2,1)} %get-tuple-element.18.pack_ref), custom_call_target="tpu_custom_call" | custom-call | tf_op jit(solution)/shard_map/finish/pallas_call | solution.py:574
Async XLA Ops:
  0.6 11.0 %copy-start.3 = (bf16[640,64]{0,1:T(8,128)(2,1)S(1)}, bf16[640,64]{0,1:T(8,128)(2,1)}, u32[]{:S(2)}) copy-start(bf16[640,64]{0,1:T(8,128)(2,1)} %param.15) | copy-start | bytes 245764
  0.6 11.0 %copy-start.4 = (s32[32,128]{1,0:T(8,128)S(1)}, s32[32,128]{1,0:T(8,128)}, u32[]{:S(2)}) copy-start(s32[32,128]{1,0:T(8,128)} %nbr_ref.1) | copy-start | bytes 49156
  0.7 11.0 %copy-start.5 = (s32[32,128]{1,0:T(8,128)S(1)}, s32[32,128]{1,0:T(8,128)}, u32[]{:S(2)}) copy-start(s32[32,128]{1,0:T(8,128)} %valid_ref.1) | copy-start | bytes 49156
  0.7 11.0 %copy-start.6 = (f32[64,8]{0,1:T(8,128)S(1)}, f32[64,8]{0,1:T(8,128)}, u32[]{:S(2)}) copy-start(f32[64,8]{0,1:T(8,128)} %param.14) | copy-start | bytes 6148
  0.7 11.0 %copy-start.7 = (f32[5,128]{1,0:T(8,128)S(1)}, f32[5,128]{1,0:T(8,128)}, u32[]{:S(2)}) copy-start(f32[5,128]{1,0:T(8,128)} %read_ref.1) | copy-start | bytes 7684
  0.7 11.0 %copy-start.8 = (bf16[3,128]{1,0:T(4,128)(2,1)S(1)}, bf16[3,128]{1,0:T(4,128)(2,1)}, u32[]{:S(2)}) copy-start(bf16[3,128]{1,0:T(4,128)(2,1)} %probe_ref.1) | copy-start | bytes 2308
  0.7 11.0 %copy-start.9 = (f32[128]{0:T(128)S(1)}, f32[128]{0:T(128)}, u32[]{:S(2)}) copy-start(f32[128]{0:T(128)} %param.17) | copy-start | bytes 1540
  11.7 0.9 %copy-start = (bf16[6,144,128]{2,1,0:T(8,128)(2,1)S(1)}, bf16[6,144,128]{2,1,0:T(8,128)(2,1)}, u32[]{:S(2)}) copy-start(bf16[6,144,128]{2,1,0:T(8,128)(2,1)} %halo.1.win_ref) | copy-start | bytes 663556
  35.5 0.7 %copy-start.1 = (bf16[6,128,128]{2,1,0:T(8,128)(2,1)}, bf16[6,128,128]{2,1,0:T(8,128)(2,1)S(1)}, u32[]{:S(2)}) copy-start(bf16[6,128,128]{2,1,0:T(8,128)(2,1)S(1)} %get-tuple-element.15.gwin_ref) | copy-start | bytes 589828
  36.2 0.6 %copy-start.2 = (bf16[384,128]{1,0:T(8,128)(2,1)}, bf16[384,128]{1,0:T(8,128)(2,1)S(1)}, u32[]{:S(2)}) copy-start(bf16[384,128]{1,0:T(8,128)(2,1)S(1)} %get-tuple-element.16.pack_ref) | copy-start | bytes 294916
